TPU v7x, 512 devices: a whole 4x8x8 slice. The times are simulated.
512 devices in a mesh: enc: 2 (over y_lo), blk: 32 (over x, y_hi, core), uly: 8 (over z).
Axes of the slice: x: 4, y: 8 (y_hi: 4, y_lo: 2; y = y_hi * 2 + y_lo), z: 8, core: 2. Of those that a mesh axis runs over, the one named last changes fastest.
Arguments:
- img_query: bfloat16 [2, 14336, 2048], P('enc', ('blk', 'uly')), may hold values from -6 to 6
- img_key: bfloat16 [2, 14336, 2048], P('enc', ('blk', 'uly')), may hold values from -6 to 6
- img_value: bfloat16 [2, 14336, 2048], P('enc', ('blk', 'uly')), may hold values from -6 to 6
- text_query: bfloat16 [2, 256, 2048], P(None, ('blk', 'enc'), 'uly'), may hold values from -6 to 6
- text_key: bfloat16 [2, 256, 2048], P(None, ('blk', 'enc'), 'uly'), may hold values from -8 to 8
- text_value: bfloat16 [2, 256, 2048], P(None, ('blk', 'enc'), 'uly'), may hold values from -6 to 6
- text_len: int32 [2], P('enc'), may hold values from 85 to 256, as said below
Outputs:
- img_out: bfloat16 [2, 14336, 2048], P('enc', ('blk', 'uly'))
- text_out: bfloat16 [2, 256, 2048], P('enc', 'blk', 'uly')
Inputs may be any that keep to these rules, and one draw needn't show every extreme that they name: `text_len`: one prompt uses all 256 rows, the other 85 or more.
All inputs are finite; a program needn't handle non-finite values.
Results may differ from a plain program's by a relative error of at most 0.007.
Values may be sent and summed in bfloat16 or wider, within the bound.
No kernel may reach another device: no remote copies, remote signals or barrier semaphores. Data moves between devices by JAX's collectives and lax.ppermute only.
A program may use at most 192 MiB of HBM per device.

v0:
```python
import jax
import jax.numpy as jnp
from jax import lax
from jax.sharding import PartitionSpec as P

HD = 128


def from_behind(block, axis, distance):
    devices = range(lax.axis_size(axis))
    route = [((i - distance) % len(devices), i) for i in devices]
    return lax.ppermute(block, axis, route)


def local(img_query, img_key, img_value, text_query, text_key, text_value, text_len):
    score_scale = HD ** (-0.5)
    text_q, text_k, text_v = (
        lax.all_to_all(text_query, "enc", split_axis=0, concat_axis=1, tiled=True),
        lax.all_to_all(text_key, "enc", split_axis=0, concat_axis=1, tiled=True),
        lax.all_to_all(text_value, "enc", split_axis=0, concat_axis=1, tiled=True),
    )
    local_q, local_k, local_v = (
        lax.all_to_all(img_query, "uly", split_axis=2, concat_axis=1, tiled=True),
        lax.all_to_all(img_key, "uly", split_axis=2, concat_axis=1, tiled=True),
        lax.all_to_all(img_value, "uly", split_axis=2, concat_axis=1, tiled=True),
    )
    blocks = lax.axis_size("blk")
    cycle_place = lax.axis_index("blk")
    img_rows = local_q.shape[1]
    text_rows = text_q.shape[1]
    col_count = local_q.shape[2]
    local_heads = col_count // HD
    count_q = img_rows + text_rows
    text_limit = text_len[0]
    queries = jnp.concatenate([local_q, text_q], 1).reshape(1, count_q, local_heads, HD)
    softmax_state = (
        jnp.full((1, count_q, local_heads), -1e30, jnp.float32),
        jnp.zeros((1, count_q, local_heads), jnp.float32),
        jnp.zeros((1, count_q, local_heads, HD), jnp.float32),
    )

    def absorb(current, key_rows, value_rows, key_valid):
        running_max, denominator, summed = current
        key_count = key_rows.shape[1]
        key_rows = key_rows.reshape(1, key_count, local_heads, HD)
        value_rows = value_rows.reshape(1, key_count, local_heads, HD)
        scores = (
            jnp.einsum("bqhd,bkhd->bqhk", queries, key_rows, preferred_element_type=jnp.float32)
            * score_scale
        )
        key_mask = key_valid[None, None, None, :]
        scores = jnp.where(key_mask, scores, -1e30)
        new_max = jnp.maximum(running_max, jnp.max(scores, axis=-1))
        rescale = jnp.exp(running_max - new_max)
        weights = jnp.where(key_mask, jnp.exp(scores - new_max[..., None]), 0.0)
        denominator = denominator * rescale + jnp.sum(weights, axis=-1)
        summed = summed * rescale[..., None] + jnp.einsum(
            "bqhk,bkhd->bqhd",
            weights.astype(jnp.bfloat16),
            value_rows,
            preferred_element_type=jnp.float32,
        )
        return (new_max, denominator, summed)

    key_block = jnp.concatenate([local_k, text_k], 1)
    value_block = jnp.concatenate([local_v, text_v], 1)
    shard_rows = img_rows + text_rows

    def row_valid(first_row, key_count):
        whole_index = first_row + jnp.arange(key_count, dtype=jnp.int32)
        within = whole_index % shard_rows
        text_index = whole_index // shard_rows * text_rows + within - img_rows
        return (within < img_rows) | (text_index < text_limit)

    softmax_state = absorb(
        softmax_state, key_block, value_block, row_valid(cycle_place * shard_rows, shard_rows)
    )

    def cycle_turn(turn_index, loop_carry):
        current, moving_k, moving_v = loop_carry
        moving_k, moving_v = from_behind((moving_k, moving_v), "blk", 1)
        source = (cycle_place - turn_index - 1) % blocks
        current = absorb(current, moving_k, moving_v, row_valid(source * shard_rows, shard_rows))
        return (current, moving_k, moving_v)

    softmax_state = lax.fori_loop(
        0, blocks - 1, cycle_turn, (softmax_state, key_block, value_block)
    )[0]
    running_max, denominator, summed = softmax_state
    attended = (summed / denominator[..., None]).reshape(1, count_q, col_count).astype(jnp.bfloat16)
    img_out = lax.all_to_all(attended[:, :img_rows], "uly", split_axis=1, concat_axis=2, tiled=True)
    return (img_out, attended[:, img_rows:])


def solution(mesh):
    placed = (
        P("enc", ("blk", "uly"), None),
        P("enc", ("blk", "uly"), None),
        P("enc", ("blk", "uly"), None),
        P(None, ("blk", "enc"), "uly"),
        P(None, ("blk", "enc"), "uly"),
        P(None, ("blk", "enc"), "uly"),
        P("enc"),
    )
    return jax.shard_map(
        local,
        mesh=mesh,
        in_specs=placed,
        out_specs=(P("enc", ("blk", "uly"), None), P("enc", "blk", "uly")),
        check_vma=False,
    )
```

profile of v0, /device:TPU:8, one launch (start us, length us, event | category | flops | bytes accessed | tf_op | source)
XLA Modules:
  0.0 702.5 jit_solution(11873365515011466778)
XLA Ops:
  0.6 10.8 %all_to_all.102 = bf16[2,4,256]{2,1,0:T(4,128)(2,1)S(1)} all-to-all(bf16[2,4,256]{2,1,0:T(4,128)(2,1)} %param.12), channel_id=1, replica_groups=mesh['enc'=2,'blk'=32,'uly'=8] {'enc'}, dimensions={0} | all-to-all | bytes 8192 | tf_op jit(solution)/shard_map/all_to_all | solution.py:18
  26.4 11.5 %reduce.16 = bf16[2048,56]{1,0:T(8,128)(2,1)S(1)} reduce(bf16[2048,1,56]{2,1,0:T(2,128)(2,1)S(1)} %bitcast.187, bf16[]{:T(256)} %broadcast.329), dimensions={1}, to_apply=%bitcast.140.reduce_sub_computation | reduce | bytes 458754
  45.3 11.5 %reduce.17 = bf16[2048,56]{1,0:T(8,128)(2,1)S(1)} reduce(bf16[2048,1,56]{2,1,0:T(2,128)(2,1)S(1)} %bitcast.188, bf16[]{:T(256)} %broadcast.329), dimensions={1}, to_apply=%bitcast.138.reduce_sub_computation | reduce | bytes 458754
  67.1 11.5 %reduce.18 = bf16[2048,56]{1,0:T(8,128)(2,1)S(1)} reduce(bf16[2048,1,56]{2,1,0:T(2,128)(2,1)S(1)} %bitcast.189, bf16[]{:T(256)} %broadcast.329), dimensions={1}, to_apply=%bitcast.142.reduce_sub_computation | reduce | bytes 458754
  105.5 579.3 %while.24 = (s32[]{:T(128)}, f32[1,456,2]{1,2,0:T(2,128)S(1)}, f32[1,456,2]{1,2,0:T(2,128)S(1)}, f32[1,456,2,128]{3,1,2,0:T(8,128)S(1)}, bf16[1,456,256]{2,1,0:T...) while((s32[]{:T(128)}, f32[1,456,2]{1,2,0:T(2,128)S(1)}, ...), condition=%wide.region_5.6_spmd, body=%wide.region_2.5_spmd.sunk | while | flops 218577696 | bytes 10420886 | solution.py:86
  167.6 11.6 %collective-permute-done = bf16[1,456,256]{2,1,0:T(8,128)(2,1)S(1)} collective-permute-done((bf16[1,456,256]{2,1,0:T(8,128)(2,1)S(1)}, bf16[1,456,256]{2,1,0:T(8,128)(2,1)S(1)}, u32[]{:S(2)}, u32[]{:S(2)}) %collective-permute-start) | collective-permute-done | bytes 233504 | tf_op jit(solution)/shard_map/while/body/eval_jaxpr/ppermute | solution.py:12
  188.1 10.0 %collective-permute-done = bf16[1,456,256]{2,1,0:T(8,128)(2,1)S(1)} collective-permute-done((bf16[1,456,256]{2,1,0:T(8,128)(2,1)S(1)}, bf16[1,456,256]{2,1,0:T(8,128)(2,1)S(1)}, u32[]{:S(2)}, u32[]{:S(2)}) %collective-permute-start) | collective-permute-done | bytes 233504 | tf_op jit(solution)/shard_map/while/body/eval_jaxpr/ppermute | solution.py:12
  207.0 9.6 %collective-permute-done = bf16[1,456,256]{2,1,0:T(8,128)(2,1)S(1)} collective-permute-done((bf16[1,456,256]{2,1,0:T(8,128)(2,1)S(1)}, bf16[1,456,256]{2,1,0:T(8,128)(2,1)S(1)}, u32[]{:S(2)}, u32[]{:S(2)}) %collective-permute-start) | collective-permute-done | bytes 233504 | tf_op jit(solution)/shard_map/while/body/eval_jaxpr/ppermute | solution.py:12
  225.6 9.7 %collective-permute-done = bf16[1,456,256]{2,1,0:T(8,128)(2,1)S(1)} collective-permute-done((bf16[1,456,256]{2,1,0:T(8,128)(2,1)S(1)}, bf16[1,456,256]{2,1,0:T(8,128)(2,1)S(1)}, u32[]{:S(2)}, u32[]{:S(2)}) %collective-permute-start) | collective-permute-done | bytes 233504 | tf_op jit(solution)/shard_map/while/body/eval_jaxpr/ppermute | solution.py:12
  244.1 9.6 %collective-permute-done = bf16[1,456,256]{2,1,0:T(8,128)(2,1)S(1)} collective-permute-done((bf16[1,456,256]{2,1,0:T(8,128)(2,1)S(1)}, bf16[1,456,256]{2,1,0:T(8,128)(2,1)S(1)}, u32[]{:S(2)}, u32[]{:S(2)}) %collective-permute-start) | collective-permute-done | bytes 233504 | tf_op jit(solution)/shard_map/while/body/eval_jaxpr/ppermute | solution.py:12
  262.6 9.8 %collective-permute-done = bf16[1,456,256]{2,1,0:T(8,128)(2,1)S(1)} collective-permute-done((bf16[1,456,256]{2,1,0:T(8,128)(2,1)S(1)}, bf16[1,456,256]{2,1,0:T(8,128)(2,1)S(1)}, u32[]{:S(2)}, u32[]{:S(2)}) %collective-permute-start) | collective-permute-done | bytes 233504 | tf_op jit(solution)/shard_map/while/body/eval_jaxpr/ppermute | solution.py:12
  299.3 9.8 %collective-permute-done = bf16[1,456,256]{2,1,0:T(8,128)(2,1)S(1)} collective-permute-done((bf16[1,456,256]{2,1,0:T(8,128)(2,1)S(1)}, bf16[1,456,256]{2,1,0:T(8,128)(2,1)S(1)}, u32[]{:S(2)}, u32[]{:S(2)}) %collective-permute-start) | collective-permute-done | bytes 233504 | tf_op jit(solution)/shard_map/while/body/eval_jaxpr/ppermute | solution.py:12
  335.9 9.6 %collective-permute-done = bf16[1,456,256]{2,1,0:T(8,128)(2,1)S(1)} collective-permute-done((bf16[1,456,256]{2,1,0:T(8,128)(2,1)S(1)}, bf16[1,456,256]{2,1,0:T(8,128)(2,1)S(1)}, u32[]{:S(2)}, u32[]{:S(2)}) %collective-permute-start) | collective-permute-done | bytes 233504 | tf_op jit(solution)/shard_map/while/body/eval_jaxpr/ppermute | solution.py:12
  354.4 9.6 %collective-permute-done = bf16[1,456,256]{2,1,0:T(8,128)(2,1)S(1)} collective-permute-done((bf16[1,456,256]{2,1,0:T(8,128)(2,1)S(1)}, bf16[1,456,256]{2,1,0:T(8,128)(2,1)S(1)}, u32[]{:S(2)}, u32[]{:S(2)}) %collective-permute-start) | collective-permute-done | bytes 233504 | tf_op jit(solution)/shard_map/while/body/eval_jaxpr/ppermute | solution.py:12
  372.8 9.5 %collective-permute-done = bf16[1,456,256]{2,1,0:T(8,128)(2,1)S(1)} collective-permute-done((bf16[1,456,256]{2,1,0:T(8,128)(2,1)S(1)}, bf16[1,456,256]{2,1,0:T(8,128)(2,1)S(1)}, u32[]{:S(2)}, u32[]{:S(2)}) %collective-permute-start) | collective-permute-done | bytes 233504 | tf_op jit(solution)/shard_map/while/body/eval_jaxpr/ppermute | solution.py:12
  391.2 9.7 %collective-permute-done = bf16[1,456,256]{2,1,0:T(8,128)(2,1)S(1)} collective-permute-done((bf16[1,456,256]{2,1,0:T(8,128)(2,1)S(1)}, bf16[1,456,256]{2,1,0:T(8,128)(2,1)S(1)}, u32[]{:S(2)}, u32[]{:S(2)}) %collective-permute-start) | collective-permute-done | bytes 233504 | tf_op jit(solution)/shard_map/while/body/eval_jaxpr/ppermute | solution.py:12
  409.7 10.2 %collective-permute-done = bf16[1,456,256]{2,1,0:T(8,128)(2,1)S(1)} collective-permute-done((bf16[1,456,256]{2,1,0:T(8,128)(2,1)S(1)}, bf16[1,456,256]{2,1,0:T(8,128)(2,1)S(1)}, u32[]{:S(2)}, u32[]{:S(2)}) %collective-permute-start) | collective-permute-done | bytes 233504 | tf_op jit(solution)/shard_map/while/body/eval_jaxpr/ppermute | solution.py:12
  428.8 10.9 %collective-permute-done = bf16[1,456,256]{2,1,0:T(8,128)(2,1)S(1)} collective-permute-done((bf16[1,456,256]{2,1,0:T(8,128)(2,1)S(1)}, bf16[1,456,256]{2,1,0:T(8,128)(2,1)S(1)}, u32[]{:S(2)}, u32[]{:S(2)}) %collective-permute-start) | collective-permute-done | bytes 233504 | tf_op jit(solution)/shard_map/while/body/eval_jaxpr/ppermute | solution.py:12
  448.6 9.7 %collective-permute-done = bf16[1,456,256]{2,1,0:T(8,128)(2,1)S(1)} collective-permute-done((bf16[1,456,256]{2,1,0:T(8,128)(2,1)S(1)}, bf16[1,456,256]{2,1,0:T(8,128)(2,1)S(1)}, u32[]{:S(2)}, u32[]{:S(2)}) %collective-permute-start) | collective-permute-done | bytes 233504 | tf_op jit(solution)/shard_map/while/body/eval_jaxpr/ppermute | solution.py:12
  467.3 9.6 %collective-permute-done = bf16[1,456,256]{2,1,0:T(8,128)(2,1)S(1)} collective-permute-done((bf16[1,456,256]{2,1,0:T(8,128)(2,1)S(1)}, bf16[1,456,256]{2,1,0:T(8,128)(2,1)S(1)}, u32[]{:S(2)}, u32[]{:S(2)}) %collective-permute-start) | collective-permute-done | bytes 233504 | tf_op jit(solution)/shard_map/while/body/eval_jaxpr/ppermute | solution.py:12
  485.8 9.5 %collective-permute-done = bf16[1,456,256]{2,1,0:T(8,128)(2,1)S(1)} collective-permute-done((bf16[1,456,256]{2,1,0:T(8,128)(2,1)S(1)}, bf16[1,456,256]{2,1,0:T(8,128)(2,1)S(1)}, u32[]{:S(2)}, u32[]{:S(2)}) %collective-permute-start) | collective-permute-done | bytes 233504 | tf_op jit(solution)/shard_map/while/body/eval_jaxpr/ppermute | solution.py:12
  504.3 9.6 %collective-permute-done = bf16[1,456,256]{2,1,0:T(8,128)(2,1)S(1)} collective-permute-done((bf16[1,456,256]{2,1,0:T(8,128)(2,1)S(1)}, bf16[1,456,256]{2,1,0:T(8,128)(2,1)S(1)}, u32[]{:S(2)}, u32[]{:S(2)}) %collective-permute-start) | collective-permute-done | bytes 233504 | tf_op jit(solution)/shard_map/while/body/eval_jaxpr/ppermute | solution.py:12
  522.8 9.6 %collective-permute-done = bf16[1,456,256]{2,1,0:T(8,128)(2,1)S(1)} collective-permute-done((bf16[1,456,256]{2,1,0:T(8,128)(2,1)S(1)}, bf16[1,456,256]{2,1,0:T(8,128)(2,1)S(1)}, u32[]{:S(2)}, u32[]{:S(2)}) %collective-permute-start) | collective-permute-done | bytes 233504 | tf_op jit(solution)/shard_map/while/body/eval_jaxpr/ppermute | solution.py:12
  541.4 9.6 %collective-permute-done = bf16[1,456,256]{2,1,0:T(8,128)(2,1)S(1)} collective-permute-done((bf16[1,456,256]{2,1,0:T(8,128)(2,1)S(1)}, bf16[1,456,256]{2,1,0:T(8,128)(2,1)S(1)}, u32[]{:S(2)}, u32[]{:S(2)}) %collective-permute-start) | collective-permute-done | bytes 233504 | tf_op jit(solution)/shard_map/while/body/eval_jaxpr/ppermute | solution.py:12
  559.9 9.6 %collective-permute-done = bf16[1,456,256]{2,1,0:T(8,128)(2,1)S(1)} collective-permute-done((bf16[1,456,256]{2,1,0:T(8,128)(2,1)S(1)}, bf16[1,456,256]{2,1,0:T(8,128)(2,1)S(1)}, u32[]{:S(2)}, u32[]{:S(2)}) %collective-permute-start) | collective-permute-done | bytes 233504 | tf_op jit(solution)/shard_map/while/body/eval_jaxpr/ppermute | solution.py:12
  578.4 9.6 %collective-permute-done = bf16[1,456,256]{2,1,0:T(8,128)(2,1)S(1)} collective-permute-done((bf16[1,456,256]{2,1,0:T(8,128)(2,1)S(1)}, bf16[1,456,256]{2,1,0:T(8,128)(2,1)S(1)}, u32[]{:S(2)}, u32[]{:S(2)}) %collective-permute-start) | collective-permute-done | bytes 233504 | tf_op jit(solution)/shard_map/while/body/eval_jaxpr/ppermute | solution.py:12
  596.9 9.6 %collective-permute-done = bf16[1,456,256]{2,1,0:T(8,128)(2,1)S(1)} collective-permute-done((bf16[1,456,256]{2,1,0:T(8,128)(2,1)S(1)}, bf16[1,456,256]{2,1,0:T(8,128)(2,1)S(1)}, u32[]{:S(2)}, u32[]{:S(2)}) %collective-permute-start) | collective-permute-done | bytes 233504 | tf_op jit(solution)/shard_map/while/body/eval_jaxpr/ppermute | solution.py:12
  615.5 9.6 %collective-permute-done = bf16[1,456,256]{2,1,0:T(8,128)(2,1)S(1)} collective-permute-done((bf16[1,456,256]{2,1,0:T(8,128)(2,1)S(1)}, bf16[1,456,256]{2,1,0:T(8,128)(2,1)S(1)}, u32[]{:S(2)}, u32[]{:S(2)}) %collective-permute-start) | collective-permute-done | bytes 233504 | tf_op jit(solution)/shard_map/while/body/eval_jaxpr/ppermute | solution.py:12
  634.0 9.6 %collective-permute-done = bf16[1,456,256]{2,1,0:T(8,128)(2,1)S(1)} collective-permute-done((bf16[1,456,256]{2,1,0:T(8,128)(2,1)S(1)}, bf16[1,456,256]{2,1,0:T(8,128)(2,1)S(1)}, u32[]{:S(2)}, u32[]{:S(2)}) %collective-permute-start) | collective-permute-done | bytes 233504 | tf_op jit(solution)/shard_map/while/body/eval_jaxpr/ppermute | solution.py:12
  652.5 9.6 %collective-permute-done = bf16[1,456,256]{2,1,0:T(8,128)(2,1)S(1)} collective-permute-done((bf16[1,456,256]{2,1,0:T(8,128)(2,1)S(1)}, bf16[1,456,256]{2,1,0:T(8,128)(2,1)S(1)}, u32[]{:S(2)}, u32[]{:S(2)}) %collective-permute-start) | collective-permute-done | bytes 233504 | tf_op jit(solution)/shard_map/while/body/eval_jaxpr/ppermute | solution.py:12
  670.9 9.6 %collective-permute-done = bf16[1,456,256]{2,1,0:T(8,128)(2,1)S(1)} collective-permute-done((bf16[1,456,256]{2,1,0:T(8,128)(2,1)S(1)}, bf16[1,456,256]{2,1,0:T(8,128)(2,1)S(1)}, u32[]{:S(2)}, u32[]{:S(2)}) %collective-permute-start) | collective-permute-done | bytes 233504 | tf_op jit(solution)/shard_map/while/body/eval_jaxpr/ppermute | solution.py:12
  692.2 9.4 %all-to-all-done.6 = bf16[8,2,7168]{2,1,0:T(2,128)(2,1)S(1)} async-done(((bf16[8,2,7168]{2,1,0:T(2,128)(2,1)}), bf16[8,2,7168]{2,1,0:T(2,128)(2,1)S(1)}, u32[]{:S(2)}, u32[]{:S(2)}) %all-to-all-start.6) | async-done | bytes 229408 | tf_op jit(solution)/shard_map/all_to_all | solution.py:91
  (506 shorter events, 389.2 us)
Async XLA Ops:
  18.4 21.2 %all-to-all-start.5 = ((bf16[2,4,256]{2,1,0:T(4,128)(2,1)}), bf16[2,4,256]{2,1,0:T(4,128)(2,1)S(1)}, u32[]{:S(2)}, u32[]{:S(2)}) async-start(bf16[2,4,256]{2,1,0:T(4,128)(2,1)} %param.14), calls=%async_computation.5 | async-start | bytes 8192 | tf_op jit(solution)/shard_map/all_to_all | solution.py:20
  39.6 18.9 %all-to-all-start.2 = ((bf16[8,2,7168]{2,1,0:T(2,128)(2,1)}), bf16[8,2,7168]{2,1,0:T(2,128)(2,1)S(1)}, u32[]{:S(2)}, u32[]{:S(2)}) async-start(bf16[8,2,7168]{2,1,0:T(2,128)(2,1)} %reshape.265), calls=%async_computation.2 | async-start | bytes 458752 | tf_op jit(solution)/shard_map/all_to_all | solution.py:23
  58.5 24.4 %all-to-all-start = ((bf16[8,2,7168]{2,1,0:T(2,128)(2,1)}), bf16[8,2,7168]{2,1,0:T(2,128)(2,1)S(1)}, u32[]{:S(2)}, u32[]{:S(2)}) async-start(bf16[8,2,7168]{2,1,0:T(2,128)(2,1)} %reshape.263), calls=%async_computation | async-start | bytes 458752 | tf_op jit(solution)/shard_map/all_to_all | solution.py:24
  82.9 17.4 %all-to-all-start.4 = ((bf16[8,2,7168]{2,1,0:T(2,128)(2,1)}), bf16[8,2,7168]{2,1,0:T(2,128)(2,1)S(1)}, u32[]{:S(2)}, u32[]{:S(2)}) async-start(bf16[8,2,7168]{2,1,0:T(2,128)(2,1)} %reshape.267), calls=%async_computation.4 | async-start | bytes 458752 | tf_op jit(solution)/shard_map/all_to_all | solution.py:25
  105.5 16.1 %collective-permute-start = (bf16[1,456,256]{2,1,0:T(8,128)(2,1)S(1)}, bf16[1,456,256]{2,1,0:T(8,128)(2,1)S(1)}, u32[]{:S(2)}, u32[]{:S(2)}) collective-permute-start(bf16[1,456,256]{2,1,0:T(8,128)(2,1)S(1)} %get-tuple-element.378), channel_id=1, source_target_pairs={{248,0},{0,8},{8,16},{16,24},{24,32},{32,40},{40,48},{48,56},{56,6... | collective-permute-start | bytes 700424 | tf_op jit(solution)/shard_map/while/body/eval_jaxpr/ppermute | solution.py:12
  107.4 16.6 %collective-permute-start.1 = (bf16[1,456,256]{2,1,0:T(8,128)(2,1)}, bf16[1,456,256]{2,1,0:T(8,128)(2,1)S(1)}, u32[]{:S(2)}, u32[]{:S(2)}) collective-permute-start(bf16[1,456,256]{2,1,0:T(8,128)(2,1)} %get-tuple-element.379), channel_id=1, source_target_pairs={{248,0},{0,8},{8,16},{16,24},{24,32},{32,40},{40,48},{48,56},{56,6... | collective-permute-start | bytes 700424 | tf_op jit(solution)/shard_map/while/body/eval_jaxpr/ppermute | solution.py:12
  144.5 16.7 %collective-permute-start.1 = (bf16[1,456,256]{2,1,0:T(8,128)(2,1)}, bf16[1,456,256]{2,1,0:T(8,128)(2,1)S(1)}, u32[]{:S(2)}, u32[]{:S(2)}) collective-permute-start(bf16[1,456,256]{2,1,0:T(8,128)(2,1)} %get-tuple-element.379), channel_id=1, source_target_pairs={{248,0},{0,8},{8,16},{16,24},{24,32},{32,40},{40,48},{48,56},{56,6... | collective-permute-start | bytes 700424 | tf_op jit(solution)/shard_map/while/body/eval_jaxpr/ppermute | solution.py:12
  163.0 16.2 %collective-permute-start = (bf16[1,456,256]{2,1,0:T(8,128)(2,1)S(1)}, bf16[1,456,256]{2,1,0:T(8,128)(2,1)S(1)}, u32[]{:S(2)}, u32[]{:S(2)}) collective-permute-start(bf16[1,456,256]{2,1,0:T(8,128)(2,1)S(1)} %get-tuple-element.378), channel_id=1, source_target_pairs={{248,0},{0,8},{8,16},{16,24},{24,32},{32,40},{40,48},{48,56},{56,6... | collective-permute-start | bytes 700424 | tf_op jit(solution)/shard_map/while/body/eval_jaxpr/ppermute | solution.py:12
  165.0 16.7 %collective-permute-start.1 = (bf16[1,456,256]{2,1,0:T(8,128)(2,1)}, bf16[1,456,256]{2,1,0:T(8,128)(2,1)S(1)}, u32[]{:S(2)}, u32[]{:S(2)}) collective-permute-start(bf16[1,456,256]{2,1,0:T(8,128)(2,1)} %get-tuple-element.379), channel_id=1, source_target_pairs={{248,0},{0,8},{8,16},{16,24},{24,32},{32,40},{40,48},{48,56},{56,6... | collective-permute-start | bytes 700424 | tf_op jit(solution)/shard_map/while/body/eval_jaxpr/ppermute | solution.py:12
  185.4 15.2 %collective-permute-start.1 = (bf16[1,456,256]{2,1,0:T(8,128)(2,1)}, bf16[1,456,256]{2,1,0:T(8,128)(2,1)S(1)}, u32[]{:S(2)}, u32[]{:S(2)}) collective-permute-start(bf16[1,456,256]{2,1,0:T(8,128)(2,1)} %get-tuple-element.379), channel_id=1, source_target_pairs={{248,0},{0,8},{8,16},{16,24},{24,32},{32,40},{40,48},{48,56},{56,6... | collective-permute-start | bytes 700424 | tf_op jit(solution)/shard_map/while/body/eval_jaxpr/ppermute | solution.py:12
  204.4 14.8 %collective-permute-start.1 = (bf16[1,456,256]{2,1,0:T(8,128)(2,1)}, bf16[1,456,256]{2,1,0:T(8,128)(2,1)S(1)}, u32[]{:S(2)}, u32[]{:S(2)}) collective-permute-start(bf16[1,456,256]{2,1,0:T(8,128)(2,1)} %get-tuple-element.379), channel_id=1, source_target_pairs={{248,0},{0,8},{8,16},{16,24},{24,32},{32,40},{40,48},{48,56},{56,6... | collective-permute-start | bytes 700424 | tf_op jit(solution)/shard_map/while/body/eval_jaxpr/ppermute | solution.py:12
  223.0 14.8 %collective-permute-start.1 = (bf16[1,456,256]{2,1,0:T(8,128)(2,1)}, bf16[1,456,256]{2,1,0:T(8,128)(2,1)S(1)}, u32[]{:S(2)}, u32[]{:S(2)}) collective-permute-start(bf16[1,456,256]{2,1,0:T(8,128)(2,1)} %get-tuple-element.379), channel_id=1, source_target_pairs={{248,0},{0,8},{8,16},{16,24},{24,32},{32,40},{40,48},{48,56},{56,6... | collective-permute-start | bytes 700424 | tf_op jit(solution)/shard_map/while/body/eval_jaxpr/ppermute | solution.py:12
  241.5 14.7 %collective-permute-start.1 = (bf16[1,456,256]{2,1,0:T(8,128)(2,1)}, bf16[1,456,256]{2,1,0:T(8,128)(2,1)S(1)}, u32[]{:S(2)}, u32[]{:S(2)}) collective-permute-start(bf16[1,456,256]{2,1,0:T(8,128)(2,1)} %get-tuple-element.379), channel_id=1, source_target_pairs={{248,0},{0,8},{8,16},{16,24},{24,32},{32,40},{40,48},{48,56},{56,6... | collective-permute-start | bytes 700424 | tf_op jit(solution)/shard_map/while/body/eval_jaxpr/ppermute | solution.py:12
  260.0 14.9 %collective-permute-start.1 = (bf16[1,456,256]{2,1,0:T(8,128)(2,1)}, bf16[1,456,256]{2,1,0:T(8,128)(2,1)S(1)}, u32[]{:S(2)}, u32[]{:S(2)}) collective-permute-start(bf16[1,456,256]{2,1,0:T(8,128)(2,1)} %get-tuple-element.379), channel_id=1, source_target_pairs={{248,0},{0,8},{8,16},{16,24},{24,32},{32,40},{40,48},{48,56},{56,6... | collective-permute-start | bytes 700424 | tf_op jit(solution)/shard_map/while/body/eval_jaxpr/ppermute | solution.py:12
  296.7 14.9 %collective-permute-start.1 = (bf16[1,456,256]{2,1,0:T(8,128)(2,1)}, bf16[1,456,256]{2,1,0:T(8,128)(2,1)S(1)}, u32[]{:S(2)}, u32[]{:S(2)}) collective-permute-start(bf16[1,456,256]{2,1,0:T(8,128)(2,1)} %get-tuple-element.379), channel_id=1, source_target_pairs={{248,0},{0,8},{8,16},{16,24},{24,32},{32,40},{40,48},{48,56},{56,6... | collective-permute-start | bytes 700424 | tf_op jit(solution)/shard_map/while/body/eval_jaxpr/ppermute | solution.py:12
  333.3 14.8 %collective-permute-start.1 = (bf16[1,456,256]{2,1,0:T(8,128)(2,1)}, bf16[1,456,256]{2,1,0:T(8,128)(2,1)S(1)}, u32[]{:S(2)}, u32[]{:S(2)}) collective-permute-start(bf16[1,456,256]{2,1,0:T(8,128)(2,1)} %get-tuple-element.379), channel_id=1, source_target_pairs={{248,0},{0,8},{8,16},{16,24},{24,32},{32,40},{40,48},{48,56},{56,6... | collective-permute-start | bytes 700424 | tf_op jit(solution)/shard_map/while/body/eval_jaxpr/ppermute | solution.py:12
  388.6 14.8 %collective-permute-start.1 = (bf16[1,456,256]{2,1,0:T(8,128)(2,1)}, bf16[1,456,256]{2,1,0:T(8,128)(2,1)S(1)}, u32[]{:S(2)}, u32[]{:S(2)}) collective-permute-start(bf16[1,456,256]{2,1,0:T(8,128)(2,1)} %get-tuple-element.379), channel_id=1, source_target_pairs={{248,0},{0,8},{8,16},{16,24},{24,32},{32,40},{40,48},{48,56},{56,6... | collective-permute-start | bytes 700424 | tf_op jit(solution)/shard_map/while/body/eval_jaxpr/ppermute | solution.py:12
  405.2 14.7 %collective-permute-start = (bf16[1,456,256]{2,1,0:T(8,128)(2,1)S(1)}, bf16[1,456,256]{2,1,0:T(8,128)(2,1)S(1)}, u32[]{:S(2)}, u32[]{:S(2)}) collective-permute-start(bf16[1,456,256]{2,1,0:T(8,128)(2,1)S(1)} %get-tuple-element.378), channel_id=1, source_target_pairs={{248,0},{0,8},{8,16},{16,24},{24,32},{32,40},{40,48},{48,56},{56,6... | collective-permute-start | bytes 700424 | tf_op jit(solution)/shard_map/while/body/eval_jaxpr/ppermute | solution.py:12
  407.1 15.3 %collective-permute-start.1 = (bf16[1,456,256]{2,1,0:T(8,128)(2,1)}, bf16[1,456,256]{2,1,0:T(8,128)(2,1)S(1)}, u32[]{:S(2)}, u32[]{:S(2)}) collective-permute-start(bf16[1,456,256]{2,1,0:T(8,128)(2,1)} %get-tuple-element.379), channel_id=1, source_target_pairs={{248,0},{0,8},{8,16},{16,24},{24,32},{32,40},{40,48},{48,56},{56,6... | collective-permute-start | bytes 700424 | tf_op jit(solution)/shard_map/while/body/eval_jaxpr/ppermute | solution.py:12
  424.3 15.4 %collective-permute-start = (bf16[1,456,256]{2,1,0:T(8,128)(2,1)S(1)}, bf16[1,456,256]{2,1,0:T(8,128)(2,1)S(1)}, u32[]{:S(2)}, u32[]{:S(2)}) collective-permute-start(bf16[1,456,256]{2,1,0:T(8,128)(2,1)S(1)} %get-tuple-element.378), channel_id=1, source_target_pairs={{248,0},{0,8},{8,16},{16,24},{24,32},{32,40},{40,48},{48,56},{56,6... | collective-permute-start | bytes 700424 | tf_op jit(solution)/shard_map/while/body/eval_jaxpr/ppermute | solution.py:12
  426.2 16.1 %collective-permute-start.1 = (bf16[1,456,256]{2,1,0:T(8,128)(2,1)}, bf16[1,456,256]{2,1,0:T(8,128)(2,1)S(1)}, u32[]{:S(2)}, u32[]{:S(2)}) collective-permute-start(bf16[1,456,256]{2,1,0:T(8,128)(2,1)} %get-tuple-element.379), channel_id=1, source_target_pairs={{248,0},{0,8},{8,16},{16,24},{24,32},{32,40},{40,48},{48,56},{56,6... | collective-permute-start | bytes 700424 | tf_op jit(solution)/shard_map/while/body/eval_jaxpr/ppermute | solution.py:12
  446.0 14.9 %collective-permute-start.1 = (bf16[1,456,256]{2,1,0:T(8,128)(2,1)}, bf16[1,456,256]{2,1,0:T(8,128)(2,1)S(1)}, u32[]{:S(2)}, u32[]{:S(2)}) collective-permute-start(bf16[1,456,256]{2,1,0:T(8,128)(2,1)} %get-tuple-element.379), channel_id=1, source_target_pairs={{248,0},{0,8},{8,16},{16,24},{24,32},{32,40},{40,48},{48,56},{56,6... | collective-permute-start | bytes 700424 | tf_op jit(solution)/shard_map/while/body/eval_jaxpr/ppermute | solution.py:12
  464.6 14.8 %collective-permute-start.1 = (bf16[1,456,256]{2,1,0:T(8,128)(2,1)}, bf16[1,456,256]{2,1,0:T(8,128)(2,1)S(1)}, u32[]{:S(2)}, u32[]{:S(2)}) collective-permute-start(bf16[1,456,256]{2,1,0:T(8,128)(2,1)} %get-tuple-element.379), channel_id=1, source_target_pairs={{248,0},{0,8},{8,16},{16,24},{24,32},{32,40},{40,48},{48,56},{56,6... | collective-permute-start | bytes 700424 | tf_op jit(solution)/shard_map/while/body/eval_jaxpr/ppermute | solution.py:12
  483.2 14.7 %collective-permute-start.1 = (bf16[1,456,256]{2,1,0:T(8,128)(2,1)}, bf16[1,456,256]{2,1,0:T(8,128)(2,1)S(1)}, u32[]{:S(2)}, u32[]{:S(2)}) collective-permute-start(bf16[1,456,256]{2,1,0:T(8,128)(2,1)} %get-tuple-element.379), channel_id=1, source_target_pairs={{248,0},{0,8},{8,16},{16,24},{24,32},{32,40},{40,48},{48,56},{56,6... | collective-permute-start | bytes 700424 | tf_op jit(solution)/shard_map/while/body/eval_jaxpr/ppermute | solution.py:12
  501.7 14.8 %collective-permute-start.1 = (bf16[1,456,256]{2,1,0:T(8,128)(2,1)}, bf16[1,456,256]{2,1,0:T(8,128)(2,1)S(1)}, u32[]{:S(2)}, u32[]{:S(2)}) collective-permute-start(bf16[1,456,256]{2,1,0:T(8,128)(2,1)} %get-tuple-element.379), channel_id=1, source_target_pairs={{248,0},{0,8},{8,16},{16,24},{24,32},{32,40},{40,48},{48,56},{56,6... | collective-permute-start | bytes 700424 | tf_op jit(solution)/shard_map/while/body/eval_jaxpr/ppermute | solution.py:12
  520.2 14.8 %collective-permute-start.1 = (bf16[1,456,256]{2,1,0:T(8,128)(2,1)}, bf16[1,456,256]{2,1,0:T(8,128)(2,1)S(1)}, u32[]{:S(2)}, u32[]{:S(2)}) collective-permute-start(bf16[1,456,256]{2,1,0:T(8,128)(2,1)} %get-tuple-element.379), channel_id=1, source_target_pairs={{248,0},{0,8},{8,16},{16,24},{24,32},{32,40},{40,48},{48,56},{56,6... | collective-permute-start | bytes 700424 | tf_op jit(solution)/shard_map/while/body/eval_jaxpr/ppermute | solution.py:12
  538.7 14.8 %collective-permute-start.1 = (bf16[1,456,256]{2,1,0:T(8,128)(2,1)}, bf16[1,456,256]{2,1,0:T(8,128)(2,1)S(1)}, u32[]{:S(2)}, u32[]{:S(2)}) collective-permute-start(bf16[1,456,256]{2,1,0:T(8,128)(2,1)} %get-tuple-element.379), channel_id=1, source_target_pairs={{248,0},{0,8},{8,16},{16,24},{24,32},{32,40},{40,48},{48,56},{56,6... | collective-permute-start | bytes 700424 | tf_op jit(solution)/shard_map/while/body/eval_jaxpr/ppermute | solution.py:12
  557.3 14.8 %collective-permute-start.1 = (bf16[1,456,256]{2,1,0:T(8,128)(2,1)}, bf16[1,456,256]{2,1,0:T(8,128)(2,1)S(1)}, u32[]{:S(2)}, u32[]{:S(2)}) collective-permute-start(bf16[1,456,256]{2,1,0:T(8,128)(2,1)} %get-tuple-element.379), channel_id=1, source_target_pairs={{248,0},{0,8},{8,16},{16,24},{24,32},{32,40},{40,48},{48,56},{56,6... | collective-permute-start | bytes 700424 | tf_op jit(solution)/shard_map/while/body/eval_jaxpr/ppermute | solution.py:12
  575.8 14.8 %collective-permute-start.1 = (bf16[1,456,256]{2,1,0:T(8,128)(2,1)}, bf16[1,456,256]{2,1,0:T(8,128)(2,1)S(1)}, u32[]{:S(2)}, u32[]{:S(2)}) collective-permute-start(bf16[1,456,256]{2,1,0:T(8,128)(2,1)} %get-tuple-element.379), channel_id=1, source_target_pairs={{248,0},{0,8},{8,16},{16,24},{24,32},{32,40},{40,48},{48,56},{56,6... | collective-permute-start | bytes 700424 | tf_op jit(solution)/shard_map/while/body/eval_jaxpr/ppermute | solution.py:12
  594.3 14.8 %collective-permute-start.1 = (bf16[1,456,256]{2,1,0:T(8,128)(2,1)}, bf16[1,456,256]{2,1,0:T(8,128)(2,1)S(1)}, u32[]{:S(2)}, u32[]{:S(2)}) collective-permute-start(bf16[1,456,256]{2,1,0:T(8,128)(2,1)} %get-tuple-element.379), channel_id=1, source_target_pairs={{248,0},{0,8},{8,16},{16,24},{24,32},{32,40},{40,48},{48,56},{56,6... | collective-permute-start | bytes 700424 | tf_op jit(solution)/shard_map/while/body/eval_jaxpr/ppermute | solution.py:12
  612.8 14.8 %collective-permute-start.1 = (bf16[1,456,256]{2,1,0:T(8,128)(2,1)}, bf16[1,456,256]{2,1,0:T(8,128)(2,1)S(1)}, u32[]{:S(2)}, u32[]{:S(2)}) collective-permute-start(bf16[1,456,256]{2,1,0:T(8,128)(2,1)} %get-tuple-element.379), channel_id=1, source_target_pairs={{248,0},{0,8},{8,16},{16,24},{24,32},{32,40},{40,48},{48,56},{56,6... | collective-permute-start | bytes 700424 | tf_op jit(solution)/shard_map/while/body/eval_jaxpr/ppermute | solution.py:12
  631.4 14.8 %collective-permute-start.1 = (bf16[1,456,256]{2,1,0:T(8,128)(2,1)}, bf16[1,456,256]{2,1,0:T(8,128)(2,1)S(1)}, u32[]{:S(2)}, u32[]{:S(2)}) collective-permute-start(bf16[1,456,256]{2,1,0:T(8,128)(2,1)} %get-tuple-element.379), channel_id=1, source_target_pairs={{248,0},{0,8},{8,16},{16,24},{24,32},{32,40},{40,48},{48,56},{56,6... | collective-permute-start | bytes 700424 | tf_op jit(solution)/shard_map/while/body/eval_jaxpr/ppermute | solution.py:12
  (37 other events, 533.1 us)
where the time goes:
time: 705 us; the launch traced here: 703 us
  waiting for transfers between devices  360 us (51%)
  starting transfers between devices  150 us (21%)
  other arithmetic  78.1 us (11%)
  matrix products  47.8 us (7%)
  local copies, waits for them, and re-layouts  44.7 us (6%)
  blocking collectives  17.8 us (3%)
    ppermute x62, waiting for transfers between devices, from_behind(): return lax.ppermute(block, axis, route)  343 us
    ppermute x62, starting transfers between devices, from_behind(): return lax.ppermute(block, axis, route)  122 us
    unnamed x4, other arithmetic  36.6 us
    dot_general x32, matrix products, absorb(): jnp.einsum('bqhk,bkhd->bqhd', weights.astype(jnp.bfloat16), value_rows, p...  32.8 us
    while x93, local copies, waits for them, and re-layouts  21.7 us
    or x32, other arithmetic, row_valid(): return (within < img_rows) | (text_index < text_limit)  20.8 us
    reduce_sum x32, other arithmetic, absorb(): denominator = denominator * rescale + jnp.sum(weights, axis=-1)  18.8 us
    unnamed x21, local copies, waits for them, and re-layouts  15.4 us
  transfers between devices with their start and end apart: 67, of which 64 were waited for; matrix products, arithmetic and copies ran while one was open for 15% of the time, Pallas kernels for 0%

commit v1 on v0

v1 whole, which is shorter than its diff:
```python
import jax
import jax.numpy as jnp
import numpy as np
from jax import lax
from jax.experimental import pallas as pl
from jax.experimental.pallas import tpu as pltpu
from jax.sharding import Mesh, PartitionSpec as P

HD = 128
HEADS = 16
ROWS = 56
TROWS = 8
GROUP = ROWS + TROWS
IMG = HEADS * ROWS
TXT = 4 * TROWS
BLOCK = IMG + TXT
LOG2_SCALE = float(HD ** -0.5 * np.log2(np.e))
MASKED = -1e30
AXES = ("enc", "x", "ya", "yb", "core", "za", "zb")
HEAD_AXES = ("za", "ya", "yb")
BF16, F32 = jnp.bfloat16, jnp.float32

VMEM = pl.BlockSpec(memory_space=pltpu.VMEM)
SMEM = pl.BlockSpec(memory_space=pltpu.SMEM)


def call(kernel, outs, args, name, flops=0, scratch=(), limit=48):
    size = sum(int(np.prod(a.shape)) * a.dtype.itemsize for a in args)
    size += sum(int(np.prod(o.shape)) * o.dtype.itemsize for o in outs)
    return pl.pallas_call(
        kernel,
        in_specs=[SMEM if a.dtype == jnp.int32 else VMEM for a in args],
        out_specs=[VMEM] * len(outs),
        out_shape=outs,
        scratch_shapes=list(scratch),
        compiler_params=pltpu.CompilerParams(vmem_limit_bytes=limit * 2**20),
        cost_estimate=pl.CostEstimate(flops=flops, bytes_accessed=size, transcendentals=0),
        name=name,
    )(*args)


def pack_kernel(place, text, query, key, value, out):
    z = place[0]
    for head in range(HEADS):
        here = (z == head // 2).astype(F32)
        columns = slice(head * HD, (head + 1) * HD)
        half = slice((head % 2) * HD, (head % 2 + 1) * HD)
        for part, rows in enumerate((query, key, value)):
            both = jnp.concatenate(
                [rows[0, :, columns].astype(F32), text[part, :, half].astype(F32) * here], 0
            )
            out[head, part * GROUP : (part + 1) * GROUP, :] = both.astype(BF16)


def unpack_kernel(place, chunks, query, kv):
    za = place[0]
    for part in range(3):
        dest = query if part == 0 else kv.at[part - 1]
        rows = slice(part * GROUP, (part + 1) * GROUP)
        for pair in range(HEADS // 2):
            two = [chunks[2 * pair + i, rows, :].astype(F32)[:ROWS] for i in range(2)]
            dest[2 * ROWS * pair : 2 * ROWS * (pair + 1), :] = jnp.concatenate(two, 0).astype(BF16)
        text = [chunks[4 * za + y, rows, :].astype(F32)[ROWS:] for y in range(4)]
        dest[IMG:BLOCK, :] = jnp.concatenate(text, 0).astype(BF16)


def flash_kernel(place, query, kv0, kv1, kv2, kv3, out, lse, text_k, text_v):
    tile = BLOCK // 2
    x, has_text, text_len = place[0], place[1], place[2]
    blocks = [(kv, core) for kv in (kv0, kv1, kv2, kv3) for core in range(2)]
    for i, (kv, core) in enumerate(blocks):
        text_k[TXT * i : TXT * (i + 1), :] = kv[core, 0, IMG:BLOCK, :]
        text_v[TXT * i : TXT * (i + 1), :] = kv[core, 1, IMG:BLOCK, :]
    column = lax.broadcasted_iota(jnp.int32, (1, TXT * len(blocks)), 1)
    from_x = (x - (column >> 6)) & 3
    index = (((from_x * 4 + ((column >> 3) & 3)) * 2 + ((column >> 5) & 1)) << 3) + (column & 7)
    limit = jnp.where(has_text > 0, text_len, 0)
    bias = jnp.where(index < limit, 0.0, MASKED)

    keys = [lambda kv=kv, core=core: kv[core, 0, :IMG, :] for kv, core in blocks] + [lambda: text_k[...]]
    values = [lambda kv=kv, core=core: kv[core, 1, :IMG, :] for kv, core in blocks] + [lambda: text_v[...]]

    def one_tile(step, carry):
        rows = pl.ds(pl.multiple_of(step * tile, 16), tile)
        q = query[rows, :]

        def score(i):
            return lax.dot_general(
                q, keys[i](), (((1,), (1,)), ((), ())), preferred_element_type=F32
            )

        top = jnp.full((tile, 1), MASKED, F32)
        both = jnp.zeros((tile, 2 * HD), F32)
        later = score(0)
        for i in range(len(keys)):
            s = later
            if i + 1 < len(keys):
                later = score(i + 1)
            if i == len(blocks):
                s = s + bias
            new_top = jnp.maximum(top, jnp.max(s, axis=1, keepdims=True))
            rescale = jnp.exp2((top - new_top) * LOG2_SCALE)
            weights = jnp.exp2((s - new_top) * LOG2_SCALE)
            v = values[i]()
            v = jnp.concatenate([v, jnp.ones(v.shape, BF16)], 1)
            both = both * rescale + jnp.dot(weights.astype(BF16), v, preferred_element_type=F32)
            top = new_top
        total = both[:, HD : HD + 1]
        out[rows, :] = (both[:, :HD] / total).astype(out.dtype)
        lse[rows, :] = jnp.broadcast_to(top * LOG2_SCALE + jnp.log2(total), (tile, HD))
        return carry

    lax.fori_loop(0, 2, one_tile, 0)


def lse_kernel(lse, out):
    out[...] = lse[...].T[:8]


def merge_kernel(place, out_a, lse_a, out_b, lse_b, chunks):
    za = place[0]
    a = lse_a[...]
    b = jnp.broadcast_to(lse_b[0:1, :], (HD, BLOCK)).T
    top = jnp.maximum(a, b)
    weight_a, weight_b = jnp.exp2(a - top), jnp.exp2(b - top)
    merged = (out_a[...] * weight_a + out_b[...].astype(F32) * weight_b) / (weight_a + weight_b)
    for source in range(HEADS):
        y = source % 4
        here = (za == source // 4).astype(F32)
        rows = [merged[ROWS * source : ROWS * (source + 1)], merged[IMG + TROWS * y : IMG + TROWS * (y + 1)] * here]
        chunks[source, :, :] = jnp.concatenate(rows, 0).astype(BF16)


def spread_kernel(place, chunks, img, text):
    z = place[0]
    for head in range(HEADS):
        img[0, :, head * HD : (head + 1) * HD] = chunks[head, :, :].astype(F32)[:ROWS].astype(BF16)
    for half in range(2):
        text[0, :, half * HD : (half + 1) * HD] = chunks[2 * z + half, :, :].astype(F32)[ROWS:].astype(BF16)


def shape(*dims, dtype=BF16):
    return jax.ShapeDtypeStruct(dims, dtype)


def shift(rows, axis, by):
    n = lax.axis_size(axis)
    return lax.ppermute(rows, axis, [(i, (i + by) % n) for i in range(n)])


def local(img_query, img_key, img_value, text_query, text_key, text_value, text_len):
    enc, x = lax.axis_index("enc"), lax.axis_index("x")
    za, zb = lax.axis_index("za"), lax.axis_index("zb")
    yh = lax.axis_index(("ya", "yb"))
    z = za * 2 + zb

    def scalars(*values):
        return jnp.stack([jnp.asarray(v, jnp.int32) for v in values])

    texts = jnp.stack([text_query, text_key, text_value])
    mine = lax.dynamic_index_in_dim(texts, enc, 1, keepdims=False)
    away = lax.dynamic_index_in_dim(texts, 1 - enc, 1, keepdims=False)
    got = shift(away, "enc", 1)
    text = jnp.where(
        enc == 0, jnp.concatenate([mine, got], 1), jnp.concatenate([got, mine], 1)
    )
    (chunks,) = call(
        pack_kernel,
        [shape(HEADS, 3 * GROUP, HD)],
        [scalars(z), text, img_query, img_key, img_value],
        "pack",
    )
    chunks = lax.all_to_all(chunks, HEAD_AXES, 0, 0, tiled=True)
    query, kv = call(
        unpack_kernel, [shape(BLOCK, HD), shape(2, BLOCK, HD)], [scalars(za), chunks], "unpack"
    )
    kvs = [kv, shift(kv, "x", 1), shift(kv, "x", 2), shift(kv, "x", -1)]
    other = shift(query, "zb", 1)
    kvs = [lax.all_gather(one, "core") for one in kvs]

    place = scalars(x, (zb == yh // 2), text_len[0])

    def flash(rows, dtype, name):
        return call(
            flash_kernel,
            [shape(BLOCK, HD, dtype=dtype), shape(BLOCK, HD, dtype=F32)],
            [place, rows, *kvs],
            name,
            flops=4 * BLOCK * 8 * BLOCK * HD,
            scratch=[pltpu.VMEM((8 * TXT, HD), BF16)] * 2,
        )

    away_out, away_lse = flash(other, BF16, "flash_other")
    (away_lse,) = call(lse_kernel, [shape(8, BLOCK, dtype=F32)], [away_lse], "lse")
    got_out, got_lse = shift(away_out, "zb", 1), shift(away_lse, "zb", 1)
    own_out, own_lse = flash(query, F32, "flash_own")
    (chunks,) = call(
        merge_kernel,
        [shape(HEADS, GROUP, HD)],
        [scalars(za), own_out, own_lse, got_out, got_lse],
        "merge",
    )
    chunks = lax.all_to_all(chunks, HEAD_AXES, 0, 0, tiled=True)
    return tuple(
        call(spread_kernel, [shape(1, ROWS, HEADS * HD), shape(1, TROWS, 2 * HD)], [scalars(z), chunks], "spread")
    )


def solution(mesh):
    fine = Mesh(mesh.devices.reshape(2, 4, 2, 2, 2, 4, 2), AXES)
    img = P("enc", AXES[1:], None)
    text = P(None, ("x", "ya", "yb", "core", "enc"), ("za", "zb"))
    return jax.shard_map(
        local,
        mesh=fine,
        in_specs=(img, img, img, text, text, text, P("enc")),
        out_specs=(img, P("enc", ("x", "ya", "yb", "core"), ("za", "zb"))),
        check_vma=False,
    )
```

time: 705 us -> 132 us (0.19)
  the two profiles are of different devices: /device:TPU:8 before, /device:TPU:2 now
where the time goes in v1:
time: 132 us; the launch traced here: 131 us
  blocking collectives  71 us (54%)
  starting transfers between devices  23.5 us (18%)
  Pallas kernels  23.4 us (18%)
  waiting for transfers between devices  7.95 us (6%)
  local copies, waits for them, and re-layouts  3.52 us (3%)
  between operations  1.47 us (1%)
    all_to_all x2, blocking collectives, local(): chunks = lax.all_to_all(chunks, HEAD_AXES, 0, 0, tiled=True)  61.1 us
    ppermute x7, starting transfers between devices, shift(): return lax.ppermute(rows, axis, [(i, (i + by) % n) for i in range(n)])  23.5 us
    pallas_call x7, Pallas kernels, call(): pl.pallas_call(kernel, in_specs=[SMEM if a.dtype == jnp.int32 else VMEM f...  23.4 us
    all_gather x4, blocking collectives, local(): kvs = [lax.all_gather(one, 'core') for one in kvs]  9.91 us
    ppermute x7, waiting for transfers between devices, shift(): return lax.ppermute(rows, axis, [(i, (i + by) % n) for i in range(n)])  7.95 us
    unnamed x12, local copies, waits for them, and re-layouts  3.5 us
  transfers between devices with their start and end apart: 7, of which 3 were waited for; matrix products, arithmetic and copies ran while one was open for 0% of the time, Pallas kernels for 8%

profile of v1, /device:TPU:2, one launch (start us, length us, event | category | flops | bytes accessed | tf_op | source)
XLA Modules:
  0.0 131.0 jit_solution(6251664471921511962)
XLA Ops:
  0.7 0.7 copy-done.5
  1.3 0.0 copy-done.4
  1.3 0.0 copy-done.3
  1.4 3.5 %collective-permute-start = (bf16[3,4,256]{2,1,0:T(4,128)(2,1)S(1)}, bf16[3,4,256]{2,1,0:T(4,128)(2,1)S(1)}, u32[]{:S(2)}, u32[]{:S(2)}) collective-permute-start(bf16[3,4,256]{2,1,0:T(4,128)(2,1)S(1)} %get-tuple-element.15), channel_id=1, source_target_pairs={{0,256},{256,0},{1,257},{257,1},{2,258},{258,2},{3,259},{259,3},{4... | collective-permute-start | bytes 18440 | tf_op jit(solution)/shard_map/ppermute | solution.py:148
  4.9 2.0 %collective-permute-done = bf16[3,4,256]{2,1,0:T(4,128)(2,1)S(1)} collective-permute-done((bf16[3,4,256]{2,1,0:T(4,128)(2,1)S(1)}, bf16[3,4,256]{2,1,0:T(4,128)(2,1)S(1)}, u32[]{:S(2)}, u32[]{:S(2)}) %collective-permute-start) | collective-permute-done | bytes 6176 | tf_op jit(solution)/shard_map/ppermute | solution.py:148
  6.9 0.0 copy-start
  7.0 0.9 copy-done
  7.9 0.9 copy-done.1
  8.8 0.9 copy-done.2
  9.8 0.1 pack.1
  9.9 40.8 %all_to_all.10.chunks = bf16[16,192,128]{2,1,0:T(8,128)(2,1)S(1)} all-to-all(bf16[16,192,128]{2,1,0:T(8,128)(2,1)S(1)} %pack.1), channel_id=1, replica_groups=mesh['enc'=2,'x'=4,'ya'=2,'yb'=2,'core'=2,'za'=4,'zb'=2] {'za','ya','yb'}, dimensions={0} | all-to-all | bytes 1572864 | tf_op jit(solution)/shard_map/all_to_all | solution.py:173
  50.7 0.1 unpack.1
  50.8 3.4 %collective-permute-start.1 = (bf16[2,928,128]{2,1,0:T(8,128)(2,1)S(1)}, bf16[2,928,128]{2,1,0:T(8,128)(2,1)S(1)}, u32[]{:S(2)}, u32[]{:S(2)}) collective-permute-start(bf16[2,928,128]{2,1,0:T(8,128)(2,1)S(1)} %get-tuple-element.9), channel_id=1, source_target_pairs={{0,64},{64,128},{128,192},{192,0},{1,65},{65,129},{129,193},{193,1... | collective-permute-start | bytes 1425416 | tf_op jit(solution)/shard_map/ppermute | solution.py:148
  54.9 0.1 pad_add_fusion.place
  54.9 3.0 %collective-permute-start.2 = (bf16[2,928,128]{2,1,0:T(8,128)(2,1)S(1)}, bf16[2,928,128]{2,1,0:T(8,128)(2,1)S(1)}, u32[]{:S(2)}, u32[]{:S(2)}) collective-permute-start(bf16[2,928,128]{2,1,0:T(8,128)(2,1)S(1)} %get-tuple-element.9), channel_id=1, source_target_pairs={{0,128},{64,192},{128,0},{192,64},{1,129},{65,193},{129,1},{193,65... | collective-permute-start | bytes 1425416 | tf_op jit(solution)/shard_map/ppermute | solution.py:148
  58.0 4.1 %collective-permute-start.3 = (bf16[2,928,128]{2,1,0:T(8,128)(2,1)S(1)}, bf16[2,928,128]{2,1,0:T(8,128)(2,1)S(1)}, u32[]{:S(2)}, u32[]{:S(2)}) collective-permute-start(bf16[2,928,128]{2,1,0:T(8,128)(2,1)S(1)} %get-tuple-element.9), channel_id=1, source_target_pairs={{0,192},{64,0},{128,64},{192,128},{1,193},{65,1},{129,65},{193,129... | collective-permute-start | bytes 1425416 | tf_op jit(solution)/shard_map/ppermute | solution.py:148
  62.0 3.6 %collective-permute-start.4 = (bf16[928,128]{1,0:T(8,128)(2,1)S(1)}, bf16[928,128]{1,0:T(8,128)(2,1)S(1)}, u32[]{:S(2)}, u32[]{:S(2)}) collective-permute-start(bf16[928,128]{1,0:T(8,128)(2,1)S(1)} %get-tuple-element.8.query), channel_id=1, source_target_pairs={{0,1},{1,0},{2,3},{3,2},{4,5},{5,4},{6,7},{7,6},{8,9},{9,8},{10,11... | collective-permute-start | bytes 712712 | tf_op jit(solution)/shard_map/ppermute | solution.py:148
  65.6 2.5 %all-gather = bf16[4,928,128]{2,1,0:T(8,128)(2,1)S(1)} all-gather(bf16[2,928,128]{2,1,0:T(8,128)(2,1)S(1)} %get-tuple-element.9), channel_id=2, replica_groups=mesh['enc'=2,'x'=4,'ya'=2,'yb'=2,'core'=2,'za'=4,'zb'=2] {'core'}, dimensions={0}, use_global_device_ids=true | all-gather | bytes 1425408 | tf_op jit(solution)/shard_map/all_gather | solution.py:179
  68.1 2.5 %all-gather.1 = bf16[4,928,128]{2,1,0:T(8,128)(2,1)S(1)} all-gather(bf16[2,928,128]{2,1,0:T(8,128)(2,1)S(1)} %collective-permute-done.1), channel_id=3, replica_groups=mesh['enc'=2,'x'=4,'ya'=2,'yb'=2,'core'=2,'za'=4,'zb'=2] {'core'}, dimensions={0}, use_global_device_ids=true | all-gather | bytes 1425408 | tf_op jit(solution)/shard_map/all_gather | solution.py:179
  70.5 1.6 %collective-permute-done.2 = bf16[2,928,128]{2,1,0:T(8,128)(2,1)S(1)} collective-permute-done((bf16[2,928,128]{2,1,0:T(8,128)(2,1)S(1)}, bf16[2,928,128]{2,1,0:T(8,128)(2,1)S(1)}, u32[]{:S(2)}, u32[]{:S(2)}) %collective-permute-start.2) | collective-permute-done | bytes 475168 | tf_op jit(solution)/shard_map/ppermute | solution.py:148
  72.1 2.5 %all-gather.2 = bf16[4,928,128]{2,1,0:T(8,128)(2,1)S(1)} all-gather(bf16[2,928,128]{2,1,0:T(8,128)(2,1)S(1)} %collective-permute-done.2), channel_id=4, replica_groups=mesh['enc'=2,'x'=4,'ya'=2,'yb'=2,'core'=2,'za'=4,'zb'=2] {'core'}, dimensions={0}, use_global_device_ids=true | all-gather | bytes 1425408 | tf_op jit(solution)/shard_map/all_gather | solution.py:179
  74.6 4.3 %collective-permute-done.3 = bf16[2,928,128]{2,1,0:T(8,128)(2,1)S(1)} collective-permute-done((bf16[2,928,128]{2,1,0:T(8,128)(2,1)S(1)}, bf16[2,928,128]{2,1,0:T(8,128)(2,1)S(1)}, u32[]{:S(2)}, u32[]{:S(2)}) %collective-permute-start.3) | collective-permute-done | bytes 475168 | tf_op jit(solution)/shard_map/ppermute | solution.py:148
  79.0 2.5 %all-gather.3 = bf16[4,928,128]{2,1,0:T(8,128)(2,1)S(1)} all-gather(bf16[2,928,128]{2,1,0:T(8,128)(2,1)S(1)} %collective-permute-done.3), channel_id=5, replica_groups=mesh['enc'=2,'x'=4,'ya'=2,'yb'=2,'core'=2,'za'=4,'zb'=2] {'core'}, dimensions={0}, use_global_device_ids=true | all-gather | bytes 1425408 | tf_op jit(solution)/shard_map/all_gather | solution.py:179
  81.4 0.0 collective-permute-done.4.query
  81.4 11.1 %flash_other.1 = (bf16[928,128]{1,0:T(8,128)(2,1)S(1)}, f32[928,128]{1,0:T(8,128)S(1)}) custom-call(s32[3]{0:T(128)S(1)} %pad_add_fusion.place, bf16[928,128]{1,0:T(8,128)(2,1)S(1)} %collective-permute-done.4.query, bf16[2,2,928,128]{3,2,1,0:T(8,128)(2,1)S(1)} %bitcast.15, bf16[2,2,928,128]{3,2,1,0:T(8,128)(2,1)S(1)} %bitcast.17, ...), custom_call_target="tpu_custom_call" | custom-call | flops 3527409664 | bytes 4751372 | tf_op jit(solution)/shard_map/flash_other/pallas_call | solution.py:30
  92.5 3.7 %collective-permute-start.5 = (bf16[928,128]{1,0:T(8,128)(2,1)S(1)}, bf16[928,128]{1,0:T(8,128)(2,1)S(1)}, u32[]{:S(2)}, u32[]{:S(2)}) collective-permute-start(bf16[928,128]{1,0:T(8,128)(2,1)S(1)} %get-tuple-element.12), channel_id=1, source_target_pairs={{0,1},{1,0},{2,3},{3,2},{4,5},{5,4},{6,7},{7,6},{8,9},{9,8},{10,11... | collective-permute-start | bytes 712712 | tf_op jit(solution)/shard_map/ppermute | solution.py:148
  96.3 0.1 lse.1
  96.4 2.3 %collective-permute-start.6 = (f32[8,928]{1,0:T(8,128)S(1)}, f32[8,928]{1,0:T(8,128)S(1)}, u32[]{:S(2)}, u32[]{:S(2)}) collective-permute-start(f32[8,928]{1,0:T(8,128)S(1)} %lse.1), channel_id=1, source_target_pairs={{0,1},{1,0},{2,3},{3,2},{4,5},{5,4},{6,7},{7,6},{8,9},{9,8},{10,11... | collective-permute-start | bytes 89096 | tf_op jit(solution)/shard_map/ppermute | solution.py:148
  98.7 10.9 %flash_own.1 = (f32[928,128]{1,0:T(8,128)S(1)}, f32[928,128]{1,0:T(8,128)S(1)}) custom-call(s32[3]{0:T(128)S(1)} %pad_add_fusion.place, bf16[928,128]{1,0:T(8,128)(2,1)S(1)} %get-tuple-element.8.query, bf16[2,2,928,128]{3,2,1,0:T(8,128)(2,1)S(1)} %bitcast.16, bf16[2,2,928,128]{3,2,1,0:T(8,128)(2,1)S(1)} %bitcast.18, bf16[2,2,928,128]{3,2,1,0:T(8,128)(2,1)S(1)} %bitcast.20, ...), custom_call_target="tpu_custom_call" | custom-call | flops 3527409664 | bytes 4988940 | tf_op jit(solution)/shard_map/flash_own/pallas_call | solution.py:30
  109.7 0.3 merge.1
  110.0 20.3 %all_to_all.11.chunks = bf16[16,64,128]{2,1,0:T(8,128)(2,1)S(1)} all-to-all(bf16[16,64,128]{2,1,0:T(8,128)(2,1)S(1)} %merge.1), channel_id=1, replica_groups=mesh['enc'=2,'x'=4,'ya'=2,'yb'=2,'core'=2,'za'=4,'zb'=2] {'za','ya','yb'}, dimensions={0} | all-to-all | bytes 524288 | tf_op jit(solution)/shard_map/all_to_all | solution.py:203
  130.3 0.7 spread.1
  (11 shorter events, 0.1 us)
Async XLA Ops:
  0.6 0.7 copy-start.5
  0.6 0.7 copy-start.4
  0.7 0.7 copy-start.3
  1.4 5.5 %collective-permute-start = (bf16[3,4,256]{2,1,0:T(4,128)(2,1)S(1)}, bf16[3,4,256]{2,1,0:T(4,128)(2,1)S(1)}, u32[]{:S(2)}, u32[]{:S(2)}) collective-permute-start(bf16[3,4,256]{2,1,0:T(4,128)(2,1)S(1)} %get-tuple-element.15), channel_id=1, source_target_pairs={{0,256},{256,0},{1,257},{257,1},{2,258},{258,2},{3,259},{259,3},{4... | collective-permute-start | bytes 18440 | tf_op jit(solution)/shard_map/ppermute | solution.py:148
  6.9 0.9 copy-start
  7.9 0.9 copy-start.1
  8.8 0.9 copy-start.2
  50.8 17.3 %collective-permute-start.1 = (bf16[2,928,128]{2,1,0:T(8,128)(2,1)S(1)}, bf16[2,928,128]{2,1,0:T(8,128)(2,1)S(1)}, u32[]{:S(2)}, u32[]{:S(2)}) collective-permute-start(bf16[2,928,128]{2,1,0:T(8,128)(2,1)S(1)} %get-tuple-element.9), channel_id=1, source_target_pairs={{0,64},{64,128},{128,192},{192,0},{1,65},{65,129},{129,193},{193,1... | collective-permute-start | bytes 1425416 | tf_op jit(solution)/shard_map/ppermute | solution.py:148
  54.9 17.2 %collective-permute-start.2 = (bf16[2,928,128]{2,1,0:T(8,128)(2,1)S(1)}, bf16[2,928,128]{2,1,0:T(8,128)(2,1)S(1)}, u32[]{:S(2)}, u32[]{:S(2)}) collective-permute-start(bf16[2,928,128]{2,1,0:T(8,128)(2,1)S(1)} %get-tuple-element.9), channel_id=1, source_target_pairs={{0,128},{64,192},{128,0},{192,64},{1,129},{65,193},{129,1},{193,65... | collective-permute-start | bytes 1425416 | tf_op jit(solution)/shard_map/ppermute | solution.py:148
  58.0 21.0 %collective-permute-start.3 = (bf16[2,928,128]{2,1,0:T(8,128)(2,1)S(1)}, bf16[2,928,128]{2,1,0:T(8,128)(2,1)S(1)}, u32[]{:S(2)}, u32[]{:S(2)}) collective-permute-start(bf16[2,928,128]{2,1,0:T(8,128)(2,1)S(1)} %get-tuple-element.9), channel_id=1, source_target_pairs={{0,192},{64,0},{128,64},{192,128},{1,193},{65,1},{129,65},{193,129... | collective-permute-start | bytes 1425416 | tf_op jit(solution)/shard_map/ppermute | solution.py:148
  62.0 19.4 %collective-permute-start.4 = (bf16[928,128]{1,0:T(8,128)(2,1)S(1)}, bf16[928,128]{1,0:T(8,128)(2,1)S(1)}, u32[]{:S(2)}, u32[]{:S(2)}) collective-permute-start(bf16[928,128]{1,0:T(8,128)(2,1)S(1)} %get-tuple-element.8.query), channel_id=1, source_target_pairs={{0,1},{1,0},{2,3},{3,2},{4,5},{5,4},{6,7},{7,6},{8,9},{9,8},{10,11... | collective-permute-start | bytes 712712 | tf_op jit(solution)/shard_map/ppermute | solution.py:148
  92.5 17.2 %collective-permute-start.5 = (bf16[928,128]{1,0:T(8,128)(2,1)S(1)}, bf16[928,128]{1,0:T(8,128)(2,1)S(1)}, u32[]{:S(2)}, u32[]{:S(2)}) collective-permute-start(bf16[928,128]{1,0:T(8,128)(2,1)S(1)} %get-tuple-element.12), channel_id=1, source_target_pairs={{0,1},{1,0},{2,3},{3,2},{4,5},{5,4},{6,7},{7,6},{8,9},{9,8},{10,11... | collective-permute-start | bytes 712712 | tf_op jit(solution)/shard_map/ppermute | solution.py:148
  96.4 13.3 %collective-permute-start.6 = (f32[8,928]{1,0:T(8,128)S(1)}, f32[8,928]{1,0:T(8,128)S(1)}, u32[]{:S(2)}, u32[]{:S(2)}) collective-permute-start(f32[8,928]{1,0:T(8,128)S(1)} %lse.1), channel_id=1, source_target_pairs={{0,1},{1,0},{2,3},{3,2},{4,5},{5,4},{6,7},{7,6},{8,9},{9,8},{10,11... | collective-permute-start | bytes 89096 | tf_op jit(solution)/shard_map/ppermute | solution.py:148

commit v2 on v1

v2 whole, which is shorter than its diff:
```python
import functools

import jax
import jax.numpy as jnp
import numpy as np
from jax import lax
from jax.experimental import pallas as pl
from jax.experimental.pallas import tpu as pltpu
from jax.sharding import Mesh, PartitionSpec as P

HD = 128
HEADS = 16
ROWS = 56
TROWS = 8
GROUP = ROWS + TROWS
IMG = HEADS * ROWS
TXT = 4 * TROWS
BLOCK = IMG + TXT
LOG2_SCALE = float(HD ** -0.5 * np.log2(np.e))
MASKED = -1e30
AXES = ("enc", "x", "ya", "yb", "core", "za", "zb")
HEAD_AXES = ("za", "ya", "yb")
BF16, F32 = jnp.bfloat16, jnp.float32

VMEM = pl.BlockSpec(memory_space=pltpu.VMEM)
SMEM = pl.BlockSpec(memory_space=pltpu.SMEM)


def call(kernel, outs, args, name, flops=0, scratch=(), limit=12):
    size = sum(int(np.prod(a.shape)) * a.dtype.itemsize for a in args)
    size += sum(int(np.prod(o.shape)) * o.dtype.itemsize for o in outs)
    return pl.pallas_call(
        kernel,
        in_specs=[SMEM if a.dtype == jnp.int32 else VMEM for a in args],
        out_specs=[VMEM] * len(outs),
        out_shape=outs,
        scratch_shapes=list(scratch),
        compiler_params=pltpu.CompilerParams(vmem_limit_bytes=limit * 2**20),
        cost_estimate=pl.CostEstimate(flops=flops, bytes_accessed=size, transcendentals=0),
        name=name,
    )(*args)


def pack_kernel(query, key, value, out):
    for head in range(HEADS):
        for part, rows in enumerate((query, key, value)):
            both = [rows[0, :, head * HD : (head + 1) * HD].astype(F32), jnp.zeros((TROWS, HD), F32)]
            out[head, part * GROUP : (part + 1) * GROUP, :] = jnp.concatenate(both, 0).astype(BF16)


def pack_text_kernel(place, text, chunks, out):
    z = place[0]
    out[...] = chunks[...]
    for half in range(2):
        for part in range(3):
            rows = slice(part * GROUP, (part + 1) * GROUP)
            both = [
                chunks[2 * z + half, rows, :].astype(F32)[:ROWS],
                text[part, :, half * HD : (half + 1) * HD].astype(F32),
            ]
            out[2 * z + half, rows, :] = jnp.concatenate(both, 0).astype(BF16)


def unpack_kernel(place, chunks, query, kv):
    za = place[0]
    for part in range(3):
        dest = query if part == 0 else kv.at[part - 1]
        rows = slice(part * GROUP, (part + 1) * GROUP)
        for pair in range(HEADS // 2):
            two = [chunks[2 * pair + i, rows, :].astype(F32)[:ROWS] for i in range(2)]
            dest[2 * ROWS * pair : 2 * ROWS * (pair + 1), :] = jnp.concatenate(two, 0).astype(BF16)
        text = [chunks[4 * za + y, rows, :].astype(F32)[ROWS:] for y in range(4)]
        dest[IMG:BLOCK, :] = jnp.concatenate(text, 0).astype(BF16)


def packed(out, logs):
    high = logs.astype(BF16).astype(F32)
    middle = (logs - high).astype(BF16).astype(F32)
    low = logs - high - middle
    row = lax.broadcasted_iota(jnp.int32, logs.shape, 0)
    logs = jnp.where(row == 0, high, jnp.where(row == 1, middle, low))
    return jnp.concatenate([out, logs], 0).astype(BF16)


def unpacked(both):
    parts = both[HD : HD + 16, :].astype(F32)
    return both[:HD, :].astype(F32), parts[0:1] + parts[1:2] + parts[2:3]


def flash_kernel(place, *refs, groups, own):
    queries, (near, far), refs = refs[:groups], refs[groups : groups + 2], refs[groups + 2 :]
    outs, (sums, tops) = refs[:-2], refs[-2:]
    x, text_near, text_len = place[0], place[1], place[2]
    blocks = [(kv, core) for kv in (near, far) for core in range(2)]
    column = lax.broadcasted_iota(jnp.int32, (1, IMG + 2 * TXT), 1) - IMG
    index = (((x * 4 + ((column >> 3) & 3)) * 2 + ((column >> 5) & 1)) << 3) + (column & 7)
    bias = jnp.where((column < 0) | (index < text_len), 0.0, MASKED)

    def rows_of(part, i):
        kv, core = blocks[i]
        rows = kv[core, part, :IMG, :]
        if i < len(blocks) - 1:
            return rows
        text = [
            jnp.where(text_near > 0, near[core, part, IMG:BLOCK, :], far[core, part, IMG:BLOCK, :])
            for core in range(2)
        ]
        return jnp.concatenate([rows] + text, 0)

    def score(q, i):
        return lax.dot_general(
            q, rows_of(0, i), (((1,), (1,)), ((), ())), preferred_element_type=F32
        )

    parts = 2 if groups == 1 else 1
    tile = BLOCK // parts
    work = [(group, i) for group in range(groups * parts) for i in range(len(blocks))]
    rows = [query[part * tile : (part + 1) * tile, :] for query in queries for part in range(parts)]
    later = score(rows[0], 0)
    for n, (group, i) in enumerate(work):
        if i == 0:
            top = jnp.full((tile, 1), MASKED, F32)
            both = jnp.zeros((tile, 2 * HD), F32)
        s = later
        if n + 1 < len(work):
            later = score(rows[work[n + 1][0]], work[n + 1][1])
        if i == len(blocks) - 1:
            s = s + bias
        new_top = jnp.maximum(top, jnp.max(s, axis=1, keepdims=True))
        rescale = jnp.exp2((top - new_top) * LOG2_SCALE)
        weights = jnp.exp2((s - new_top) * LOG2_SCALE)
        v = rows_of(1, i)
        v = jnp.concatenate([v, jnp.ones(v.shape, BF16)], 1)
        both = both * rescale + jnp.dot(weights.astype(BF16), v, preferred_element_type=F32)
        top = new_top
        if i < len(blocks) - 1:
            continue
        total = both[:, HD : HD + 1]
        group, part = divmod(group, parts)
        span = slice(part * tile, (part + 1) * tile)
        sums[group, span, :] = both[:, :HD] / total
        tops[group, span, :] = jnp.broadcast_to(top * LOG2_SCALE + jnp.log2(total), (tile, HD))
        if part < parts - 1:
            continue
        result, logs = sums[group].T, tops[group].T[:16]
        if own and group == groups - 1:
            outs[-2][...] = result
            outs[-1][...] = logs
        else:
            outs[group][...] = packed(result, logs)


def merge_kernel(place, own, own_log, got1, got2, got3, chunks):
    za = place[0]
    outs, logs = [own[...]], [own_log[:1]]
    for got in (got1, got2, got3):
        out, log = unpacked(got)
        outs.append(out)
        logs.append(log)
    top = jnp.maximum(jnp.maximum(logs[0], logs[1]), jnp.maximum(logs[2], logs[3]))
    weights = [jnp.exp2(log - top) for log in logs]
    total = weights[0] + weights[1] + weights[2] + weights[3]
    merged = sum(out * (weight / total) for out, weight in zip(outs, weights)).T
    for source in range(HEADS):
        y = source % 4
        here = (za == source // 4).astype(F32)
        rows = [merged[ROWS * source : ROWS * (source + 1)], merged[IMG + TROWS * y : IMG + TROWS * (y + 1)] * here]
        chunks[source, :, :] = jnp.concatenate(rows, 0).astype(BF16)


def spread_kernel(place, chunks, img, text):
    z = place[0]
    for head in range(HEADS):
        img[0, :, head * HD : (head + 1) * HD] = chunks[head, :, :].astype(F32)[:ROWS].astype(BF16)
    for half in range(2):
        text[0, :, half * HD : (half + 1) * HD] = chunks[2 * z + half, :, :].astype(F32)[ROWS:].astype(BF16)


def shape(*dims, dtype=BF16):
    return jax.ShapeDtypeStruct(dims, dtype)


def shift(rows, axis, by):
    n = lax.axis_size(axis)
    return lax.ppermute(rows, axis, [(i, (i + by) % n) for i in range(n)])


def local(img_query, img_key, img_value, text_query, text_key, text_value, text_len):
    enc, x = lax.axis_index("enc"), lax.axis_index("x")
    za, zb = lax.axis_index("za"), lax.axis_index("zb")
    yh = lax.axis_index(("ya", "yb"))
    z = za * 2 + zb

    def scalars(*values):
        return jnp.stack([jnp.asarray(v, jnp.int32) for v in values])

    texts = jnp.stack([text_query, text_key, text_value])
    mine = lax.dynamic_index_in_dim(texts, enc, 1, keepdims=False)
    away = lax.dynamic_index_in_dim(texts, 1 - enc, 1, keepdims=False)
    got = shift(away, "enc", 1)
    text = jnp.where(
        enc == 0, jnp.concatenate([mine, got], 1), jnp.concatenate([got, mine], 1)
    )
    (chunks,) = call(
        pack_kernel,
        [shape(HEADS, 3 * GROUP, HD)],
        [img_query, img_key, img_value],
        "pack",
    )
    (chunks,) = call(
        pack_text_kernel, [shape(HEADS, 3 * GROUP, HD)], [scalars(z), text, chunks], "pack_text"
    )
    chunks = lax.all_to_all(chunks, HEAD_AXES, 0, 0, tiled=True)
    query, kv = call(
        unpack_kernel, [shape(BLOCK, HD), shape(2, BLOCK, HD)], [scalars(za), chunks], "unpack"
    )
    far = shift(kv, "zb", 1)
    groups = [shift(query, "x", by) for by in (2, 1, -1)]
    near, far = lax.all_gather(kv, "core"), lax.all_gather(far, "core")
    place = scalars(x, (zb == yh // 2), text_len[0])

    def flash(name, rows, own=False):
        outs = [shape(HD + 16, BLOCK)] * (len(rows) - own)
        if own:
            outs += [shape(HD, BLOCK, dtype=F32), shape(16, BLOCK, dtype=F32)]
        return call(
            functools.partial(flash_kernel, groups=len(rows), own=own),
            outs,
            [place, *rows, near, far],
            name,
            flops=16 * len(rows) * BLOCK * BLOCK * HD,
            scratch=[pltpu.VMEM((len(rows), BLOCK, HD), F32)] * 2,
            limit=40,
        )

    away = flash("flash_two", groups[:2])
    got = [shift(rows, "x", by) for rows, by in zip(away, (-2, -1))]
    (away,) = flash("flash_third", groups[2:])
    got.append(shift(away, "x", 1))
    own, own_log = flash("flash_own", [query], own=True)
    (chunks,) = call(merge_kernel, [shape(HEADS, GROUP, HD)], [scalars(za), own, own_log, *got], "merge")
    chunks = lax.all_to_all(chunks, HEAD_AXES, 0, 0, tiled=True)
    return tuple(
        call(spread_kernel, [shape(1, ROWS, HEADS * HD), shape(1, TROWS, 2 * HD)], [scalars(z), chunks], "spread")
    )


def solution(mesh):
    fine = Mesh(mesh.devices.reshape(2, 4, 2, 2, 2, 4, 2), AXES)
    img = P("enc", AXES[1:], None)
    text = P(None, ("x", "ya", "yb", "core", "enc"), ("za", "zb"))
    return jax.shard_map(
        local,
        mesh=fine,
        in_specs=(img, img, img, text, text, text, P("enc")),
        out_specs=(img, P("enc", ("x", "ya", "yb", "core"), ("za", "zb"))),
        check_vma=False,
    )
```

time: 132 us -> 127 us (0.962)
  the two profiles are of different devices: /device:TPU:2 before, /device:TPU:10 now
where the time goes in v2:
time: 127 us; the launch traced here: 126 us
  blocking collectives  66.4 us (52%)
  starting transfers between devices  25.8 us (20%)
  Pallas kernels  24.3 us (19%)
  waiting for transfers between devices  4.85 us (4%)
  local copies, waits for them, and re-layouts  3.52 us (3%)
  between operations  1.5 us (1%)
    all_to_all x2, blocking collectives, local(): chunks = lax.all_to_all(chunks, HEAD_AXES, 0, 0, tiled=True)  61.4 us
    ppermute x8, starting transfers between devices, shift(): return lax.ppermute(rows, axis, [(i, (i + by) % n) for i in range(n)])  25.8 us
    pallas_call x8, Pallas kernels, call(): pl.pallas_call(kernel, in_specs=[SMEM if a.dtype == jnp.int32 else VMEM f...  24.3 us
    all_gather x2, blocking collectives, local(): near, far = (lax.all_gather(kv, 'core'), lax.all_gather(far, 'core'))  4.96 us
    ppermute x8, waiting for transfers between devices, shift(): return lax.ppermute(rows, axis, [(i, (i + by) % n) for i in range(n)])  4.85 us
    unnamed x12, local copies, waits for them, and re-layouts  3.5 us
  transfers between devices with their start and end apart: 8, of which 2 were waited for; matrix products, arithmetic and copies ran while one was open for 0% of the time, Pallas kernels for 18%

profile of v2, /device:TPU:10, one launch (start us, length us, event | category | flops | bytes accessed | tf_op | source)
XLA Modules:
  0.0 126.4 jit_solution(7709842371878871688)
XLA Ops:
  0.7 0.7 copy-done.5
  1.3 0.0 copy-done.4
  1.3 0.0 copy-done.3
  1.4 2.4 %collective-permute-start = (bf16[3,4,256]{2,1,0:T(4,128)(2,1)S(1)}, bf16[3,4,256]{2,1,0:T(4,128)(2,1)S(1)}, u32[]{:S(2)}, u32[]{:S(2)}) collective-permute-start(bf16[3,4,256]{2,1,0:T(4,128)(2,1)S(1)} %get-tuple-element.15), channel_id=1, source_target_pairs={{0,256},{256,0},{1,257},{257,1},{2,258},{258,2},{3,259},{259,3},{4... | collective-permute-start | bytes 18440 | tf_op jit(solution)/shard_map/ppermute | solution.py:185
  3.8 0.0 copy-start
  3.8 0.9 copy-done
  4.7 0.9 copy-done.1
  5.7 0.9 copy-done.2
  6.6 0.1 pack.1.chunks
  6.7 0.2 collective-permute-done
  6.9 0.1 pack_text.1
  7.0 41.7 %all_to_all.10.chunks = bf16[16,192,128]{2,1,0:T(8,128)(2,1)S(1)} all-to-all(bf16[16,192,128]{2,1,0:T(8,128)(2,1)S(1)} %pack_text.1), channel_id=1, replica_groups=mesh['enc'=2,'x'=4,'ya'=2,'yb'=2,'core'=2,'za'=4,'zb'=2] {'za','ya','yb'}, dimensions={0} | all-to-all | bytes 1572864 | tf_op jit(solution)/shard_map/all_to_all | solution.py:213
  48.7 0.1 unpack.1
  48.8 2.8 %collective-permute-start.1 = (bf16[2,928,128]{2,1,0:T(8,128)(2,1)S(1)}, bf16[2,928,128]{2,1,0:T(8,128)(2,1)S(1)}, u32[]{:S(2)}, u32[]{:S(2)}) collective-permute-start(bf16[2,928,128]{2,1,0:T(8,128)(2,1)S(1)} %get-tuple-element.9), channel_id=1, source_target_pairs={{0,1},{1,0},{2,3},{3,2},{4,5},{5,4},{6,7},{7,6},{8,9},{9,8},{10,11... | collective-permute-start | bytes 1425416 | tf_op jit(solution)/shard_map/ppermute | solution.py:185
  52.3 0.1 pad_add_fusion.place
  52.4 2.4 %collective-permute-start.6 = (bf16[928,128]{1,0:T(8,128)(2,1)S(1)}, bf16[928,128]{1,0:T(8,128)(2,1)S(1)}, u32[]{:S(2)}, u32[]{:S(2)}) collective-permute-start(bf16[928,128]{1,0:T(8,128)(2,1)S(1)} %get-tuple-element.8.refs_0_), channel_id=1, source_target_pairs={{0,192},{64,0},{128,64},{192,128},{1,193},{65,1},{129,65},{193,129... | collective-permute-start | bytes 712712 | tf_op jit(solution)/shard_map/ppermute | solution.py:185
  54.8 4.3 %collective-permute-start.2 = (bf16[928,128]{1,0:T(8,128)(2,1)S(1)}, bf16[928,128]{1,0:T(8,128)(2,1)S(1)}, u32[]{:S(2)}, u32[]{:S(2)}) collective-permute-start(bf16[928,128]{1,0:T(8,128)(2,1)S(1)} %get-tuple-element.8.refs_0_), channel_id=1, source_target_pairs={{0,128},{64,192},{128,0},{192,64},{1,129},{65,193},{129,1},{193,65... | collective-permute-start | bytes 712712 | tf_op jit(solution)/shard_map/ppermute | solution.py:185
  59.2 3.7 %collective-permute-start.3 = (bf16[928,128]{1,0:T(8,128)(2,1)S(1)}, bf16[928,128]{1,0:T(8,128)(2,1)S(1)}, u32[]{:S(2)}, u32[]{:S(2)}) collective-permute-start(bf16[928,128]{1,0:T(8,128)(2,1)S(1)} %get-tuple-element.8.refs_0_), channel_id=1, source_target_pairs={{0,64},{64,128},{128,192},{192,0},{1,65},{65,129},{129,193},{193,1... | collective-permute-start | bytes 712712 | tf_op jit(solution)/shard_map/ppermute | solution.py:185
  62.9 2.5 %all-gather = bf16[4,928,128]{2,1,0:T(8,128)(2,1)S(1)} all-gather(bf16[2,928,128]{2,1,0:T(8,128)(2,1)S(1)} %get-tuple-element.9), channel_id=2, replica_groups=mesh['enc'=2,'x'=4,'ya'=2,'yb'=2,'core'=2,'za'=4,'zb'=2] {'core'}, dimensions={0}, use_global_device_ids=true | all-gather | bytes 1425408 | tf_op jit(solution)/shard_map/all_gather | solution.py:219
  65.4 0.0 collective-permute-done.1
  65.4 2.5 %all-gather.1 = bf16[4,928,128]{2,1,0:T(8,128)(2,1)S(1)} all-gather(bf16[2,928,128]{2,1,0:T(8,128)(2,1)S(1)} %collective-permute-done.1), channel_id=3, replica_groups=mesh['enc'=2,'x'=4,'ya'=2,'yb'=2,'core'=2,'za'=4,'zb'=2] {'core'}, dimensions={0}, use_global_device_ids=true | all-gather | bytes 1425408 | tf_op jit(solution)/shard_map/all_gather | solution.py:219
  67.8 0.0 collective-permute-done.6.refs_0_
  67.8 6.1 %flash_third.1 = bf16[144,928]{1,0:T(8,128)(2,1)S(1)} custom-call(s32[3]{0:T(128)S(1)} %pad_add_fusion.place, bf16[928,128]{1,0:T(8,128)(2,1)S(1)} %collective-permute-done.6.refs_0_, bf16[2,2,928,128]{3,2,1,0:T(8,128)(2,1)S(1)} %bitcast.13, bf16[2,2,928,128]{3,2,1,0:T(8,128)(2,1)S(1)} %bitcast.16), custom_call_target="tpu_custom_call" | custom-call | flops 1763704832 | bytes 2405388 | tf_op jit(solution)/shard_map/flash_third/pallas_call | solution.py:32
  74.0 2.1 %collective-permute-start.7 = (bf16[144,928]{1,0:T(8,128)(2,1)S(1)}, bf16[144,928]{1,0:T(8,128)(2,1)S(1)}, u32[]{:S(2)}, u32[]{:S(2)}) collective-permute-start(bf16[144,928]{1,0:T(8,128)(2,1)S(1)} %flash_third.1), channel_id=1, source_target_pairs={{0,64},{64,128},{128,192},{192,0},{1,65},{65,129},{129,193},{193,1... | collective-permute-start | bytes 801800 | tf_op jit(solution)/shard_map/ppermute | solution.py:185
  76.1 10.7 %flash_two.1 = (bf16[144,928]{1,0:T(8,128)(2,1)S(1)}, bf16[144,928]{1,0:T(8,128)(2,1)S(1)}) custom-call(s32[3]{0:T(128)S(1)} %pad_add_fusion.place, bf16[928,128]{1,0:T(8,128)(2,1)S(1)} %collective-permute-done.2.refs_0_, bf16[928,128]{1,0:T(8,128)(2,1)S(1)} %collective-permute-done.3.refs_1_, bf16[2,2,928,128]{3,2,1,0:T(8,128)(2,1)S(1)} %bitcast.14, ...), custom_call_target="tpu_custom_call" | custom-call | flops 3527409664 | bytes 2910220 | tf_op jit(solution)/shard_map/flash_two/pallas_call | solution.py:32
  86.8 4.2 %collective-permute-start.4 = (bf16[144,928]{1,0:T(8,128)(2,1)S(1)}, bf16[144,928]{1,0:T(8,128)(2,1)S(1)}, u32[]{:S(2)}, u32[]{:S(2)}) collective-permute-start(bf16[144,928]{1,0:T(8,128)(2,1)S(1)} %get-tuple-element.12), channel_id=1, source_target_pairs={{0,128},{64,192},{128,0},{192,64},{1,129},{65,193},{129,1},{193,65... | collective-permute-start | bytes 801800 | tf_op jit(solution)/shard_map/ppermute | solution.py:185
  91.0 3.9 %collective-permute-start.5 = (bf16[144,928]{1,0:T(8,128)(2,1)S(1)}, bf16[144,928]{1,0:T(8,128)(2,1)S(1)}, u32[]{:S(2)}, u32[]{:S(2)}) collective-permute-start(bf16[144,928]{1,0:T(8,128)(2,1)S(1)} %get-tuple-element.13), channel_id=1, source_target_pairs={{0,192},{64,0},{128,64},{192,128},{1,193},{65,1},{129,65},{193,129... | collective-permute-start | bytes 801800 | tf_op jit(solution)/shard_map/ppermute | solution.py:185
  94.9 6.0 %flash_own.1 = (f32[128,928]{1,0:T(8,128)S(1)}, f32[16,928]{1,0:T(8,128)S(1)}) custom-call(s32[3]{0:T(128)S(1)} %pad_add_fusion.place, bf16[928,128]{1,0:T(8,128)(2,1)S(1)} %get-tuple-element.8.refs_0_, bf16[2,2,928,128]{3,2,1,0:T(8,128)(2,1)S(1)} %bitcast.15, bf16[2,2,928,128]{3,2,1,0:T(8,128)(2,1)S(1)} %bitcast.18), custom_call_target="tpu_custom_call" | custom-call | flops 1763704832 | bytes 2672652 | tf_op jit(solution)/shard_map/flash_own/pallas_call | solution.py:32
  101.0 4.6 %collective-permute-done.5.got2 = bf16[144,928]{1,0:T(8,128)(2,1)S(1)} collective-permute-done((bf16[144,928]{1,0:T(8,128)(2,1)S(1)}, bf16[144,928]{1,0:T(8,128)(2,1)S(1)}, u32[]{:S(2)}, u32[]{:S(2)}) %collective-permute-start.5) | collective-permute-done | bytes 267296 | tf_op jit(solution)/shard_map/ppermute | solution.py:185
  105.6 0.3 merge.1
  105.9 19.7 %all_to_all.11.chunks = bf16[16,64,128]{2,1,0:T(8,128)(2,1)S(1)} all-to-all(bf16[16,64,128]{2,1,0:T(8,128)(2,1)S(1)} %merge.1), channel_id=1, replica_groups=mesh['enc'=2,'x'=4,'ya'=2,'yb'=2,'core'=2,'za'=4,'zb'=2] {'za','ya','yb'}, dimensions={0} | all-to-all | bytes 524288 | tf_op jit(solution)/shard_map/all_to_all | solution.py:242
  125.7 0.7 spread.1
  (12 shorter events, 0.1 us)
Async XLA Ops:
  0.6 0.7 copy-start.5
  0.6 0.7 copy-start.4
  0.7 0.7 copy-start.3
  1.4 5.5 %collective-permute-start = (bf16[3,4,256]{2,1,0:T(4,128)(2,1)S(1)}, bf16[3,4,256]{2,1,0:T(4,128)(2,1)S(1)}, u32[]{:S(2)}, u32[]{:S(2)}) collective-permute-start(bf16[3,4,256]{2,1,0:T(4,128)(2,1)S(1)} %get-tuple-element.15), channel_id=1, source_target_pairs={{0,256},{256,0},{1,257},{257,1},{2,258},{258,2},{3,259},{259,3},{4... | collective-permute-start | bytes 18440 | tf_op jit(solution)/shard_map/ppermute | solution.py:185
  3.8 0.9 copy-start
  4.7 0.9 copy-start.1
  5.7 0.9 copy-start.2
  48.8 16.5 %collective-permute-start.1 = (bf16[2,928,128]{2,1,0:T(8,128)(2,1)S(1)}, bf16[2,928,128]{2,1,0:T(8,128)(2,1)S(1)}, u32[]{:S(2)}, u32[]{:S(2)}) collective-permute-start(bf16[2,928,128]{2,1,0:T(8,128)(2,1)S(1)} %get-tuple-element.9), channel_id=1, source_target_pairs={{0,1},{1,0},{2,3},{3,2},{4,5},{5,4},{6,7},{7,6},{8,9},{9,8},{10,11... | collective-permute-start | bytes 1425416 | tf_op jit(solution)/shard_map/ppermute | solution.py:185
  52.4 15.5 %collective-permute-start.6 = (bf16[928,128]{1,0:T(8,128)(2,1)S(1)}, bf16[928,128]{1,0:T(8,128)(2,1)S(1)}, u32[]{:S(2)}, u32[]{:S(2)}) collective-permute-start(bf16[928,128]{1,0:T(8,128)(2,1)S(1)} %get-tuple-element.8.refs_0_), channel_id=1, source_target_pairs={{0,192},{64,0},{128,64},{192,128},{1,193},{65,1},{129,65},{193,129... | collective-permute-start | bytes 712712 | tf_op jit(solution)/shard_map/ppermute | solution.py:185
  54.8 21.3 %collective-permute-start.2 = (bf16[928,128]{1,0:T(8,128)(2,1)S(1)}, bf16[928,128]{1,0:T(8,128)(2,1)S(1)}, u32[]{:S(2)}, u32[]{:S(2)}) collective-permute-start(bf16[928,128]{1,0:T(8,128)(2,1)S(1)} %get-tuple-element.8.refs_0_), channel_id=1, source_target_pairs={{0,128},{64,192},{128,0},{192,64},{1,129},{65,193},{129,1},{193,65... | collective-permute-start | bytes 712712 | tf_op jit(solution)/shard_map/ppermute | solution.py:185
  59.2 16.9 %collective-permute-start.3 = (bf16[928,128]{1,0:T(8,128)(2,1)S(1)}, bf16[928,128]{1,0:T(8,128)(2,1)S(1)}, u32[]{:S(2)}, u32[]{:S(2)}) collective-permute-start(bf16[928,128]{1,0:T(8,128)(2,1)S(1)} %get-tuple-element.8.refs_0_), channel_id=1, source_target_pairs={{0,64},{64,128},{128,192},{192,0},{1,65},{65,129},{129,193},{193,1... | collective-permute-start | bytes 712712 | tf_op jit(solution)/shard_map/ppermute | solution.py:185
  74.0 27.0 %collective-permute-start.7 = (bf16[144,928]{1,0:T(8,128)(2,1)S(1)}, bf16[144,928]{1,0:T(8,128)(2,1)S(1)}, u32[]{:S(2)}, u32[]{:S(2)}) collective-permute-start(bf16[144,928]{1,0:T(8,128)(2,1)S(1)} %flash_third.1), channel_id=1, source_target_pairs={{0,64},{64,128},{128,192},{192,0},{1,65},{65,129},{129,193},{193,1... | collective-permute-start | bytes 801800 | tf_op jit(solution)/shard_map/ppermute | solution.py:185
  86.8 14.1 %collective-permute-start.4 = (bf16[144,928]{1,0:T(8,128)(2,1)S(1)}, bf16[144,928]{1,0:T(8,128)(2,1)S(1)}, u32[]{:S(2)}, u32[]{:S(2)}) collective-permute-start(bf16[144,928]{1,0:T(8,128)(2,1)S(1)} %get-tuple-element.12), channel_id=1, source_target_pairs={{0,128},{64,192},{128,0},{192,64},{1,129},{65,193},{129,1},{193,65... | collective-permute-start | bytes 801800 | tf_op jit(solution)/shard_map/ppermute | solution.py:185
  91.0 14.6 %collective-permute-start.5 = (bf16[144,928]{1,0:T(8,128)(2,1)S(1)}, bf16[144,928]{1,0:T(8,128)(2,1)S(1)}, u32[]{:S(2)}, u32[]{:S(2)}) collective-permute-start(bf16[144,928]{1,0:T(8,128)(2,1)S(1)} %get-tuple-element.13), channel_id=1, source_target_pairs={{0,192},{64,0},{128,64},{192,128},{1,193},{65,1},{129,65},{193,129... | collective-permute-start | bytes 801800 | tf_op jit(solution)/shard_map/ppermute | solution.py:185

commit v3 on v2

--- a/solution.py
+++ b/solution.py
@@ -215,7 +215,7 @@
         unpack_kernel, [shape(BLOCK, HD), shape(2, BLOCK, HD)], [scalars(za), chunks], "unpack"
     )
     far = shift(kv, "zb", 1)
-    groups = [shift(query, "x", by) for by in (2, 1, -1)]
+    groups = [shift(query, "x", by) for by in (1, -1, 2)]
     near, far = lax.all_gather(kv, "core"), lax.all_gather(far, "core")
     place = scalars(x, (zb == yh // 2), text_len[0])
 
@@ -234,9 +234,9 @@
         )
 
     away = flash("flash_two", groups[:2])
-    got = [shift(rows, "x", by) for rows, by in zip(away, (-2, -1))]
+    got = [shift(rows, "x", by) for rows, by in zip(away, (-1, 1))]
     (away,) = flash("flash_third", groups[2:])
-    got.append(shift(away, "x", 1))
+    got.append(shift(away, "x", -2))
     own, own_log = flash("flash_own", [query], own=True)
     (chunks,) = call(merge_kernel, [shape(HEADS, GROUP, HD)], [scalars(za), own, own_log, *got], "merge")
     chunks = lax.all_to_all(chunks, HEAD_AXES, 0, 0, tiled=True)

time: 127 us -> 125 us (0.984)
  the two profiles are of different devices: /device:TPU:10 before, /device:TPU:8 now
where the time goes in v3:
time: 125 us; the launch traced here: 124 us
  blocking collectives  60.5 us (48%)
  starting transfers between devices  30.7 us (25%)
  Pallas kernels  24.3 us (19%)
  local copies, waits for them, and re-layouts  3.52 us (3%)
  waiting for transfers between devices  3.39 us (3%)
  between operations  1.51 us (1%)
    all_to_all x2, blocking collectives, local(): chunks = lax.all_to_all(chunks, HEAD_AXES, 0, 0, tiled=True)  55.5 us
    ppermute x8, starting transfers between devices, shift(): return lax.ppermute(rows, axis, [(i, (i + by) % n) for i in range(n)])  30.7 us
    pallas_call x8, Pallas kernels, call(): pl.pallas_call(kernel, in_specs=[SMEM if a.dtype == jnp.int32 else VMEM f...  24.3 us
    all_gather x2, blocking collectives, local(): near, far = (lax.all_gather(kv, 'core'), lax.all_gather(far, 'core'))  4.96 us
    unnamed x12, local copies, waits for them, and re-layouts  3.5 us
    ppermute x8, waiting for transfers between devices, shift(): return lax.ppermute(rows, axis, [(i, (i + by) % n) for i in range(n)])  3.39 us
  transfers between devices with their start and end apart: 8, of which 1 were waited for; matrix products, arithmetic and copies ran while one was open for 0% of the time, Pallas kernels for 19%

profile of v3, /device:TPU:8, one launch (start us, length us, event | category | flops | bytes accessed | tf_op | source)
XLA Modules:
  0.0 124.0 jit_solution(16755675122076431294)
XLA Ops:
  0.7 0.7 copy-done.5
  1.3 0.0 copy-done.4
  1.3 0.0 copy-done.3
  1.4 7.7 %collective-permute-start = (bf16[3,4,256]{2,1,0:T(4,128)(2,1)S(1)}, bf16[3,4,256]{2,1,0:T(4,128)(2,1)S(1)}, u32[]{:S(2)}, u32[]{:S(2)}) collective-permute-start(bf16[3,4,256]{2,1,0:T(4,128)(2,1)S(1)} %get-tuple-element.15), channel_id=1, source_target_pairs={{0,256},{256,0},{1,257},{257,1},{2,258},{258,2},{3,259},{259,3},{4... | collective-permute-start | bytes 18440 | tf_op jit(solution)/shard_map/ppermute | solution.py:185
  9.1 0.0 copy-start
  9.2 0.9 copy-done
  10.1 0.9 copy-done.1
  11.0 0.9 copy-done.2
  12.0 0.1 pack.1.chunks
  12.1 0.0 collective-permute-done
  12.1 0.1 pack_text.1
  12.2 36.5 %all_to_all.10.chunks = bf16[16,192,128]{2,1,0:T(8,128)(2,1)S(1)} all-to-all(bf16[16,192,128]{2,1,0:T(8,128)(2,1)S(1)} %pack_text.1), channel_id=1, replica_groups=mesh['enc'=2,'x'=4,'ya'=2,'yb'=2,'core'=2,'za'=4,'zb'=2] {'za','ya','yb'}, dimensions={0} | all-to-all | bytes 1572864 | tf_op jit(solution)/shard_map/all_to_all | solution.py:213
  48.7 0.1 unpack.1
  48.8 2.8 %collective-permute-start.1 = (bf16[2,928,128]{2,1,0:T(8,128)(2,1)S(1)}, bf16[2,928,128]{2,1,0:T(8,128)(2,1)S(1)}, u32[]{:S(2)}, u32[]{:S(2)}) collective-permute-start(bf16[2,928,128]{2,1,0:T(8,128)(2,1)S(1)} %get-tuple-element.9), channel_id=1, source_target_pairs={{0,1},{1,0},{2,3},{3,2},{4,5},{5,4},{6,7},{7,6},{8,9},{9,8},{10,11... | collective-permute-start | bytes 1425416 | tf_op jit(solution)/shard_map/ppermute | solution.py:185
  52.3 0.1 pad_add_fusion.place
  52.4 4.9 %collective-permute-start.6 = (bf16[928,128]{1,0:T(8,128)(2,1)S(1)}, bf16[928,128]{1,0:T(8,128)(2,1)S(1)}, u32[]{:S(2)}, u32[]{:S(2)}) collective-permute-start(bf16[928,128]{1,0:T(8,128)(2,1)S(1)} %get-tuple-element.8.refs_0_), channel_id=1, source_target_pairs={{0,128},{64,192},{128,0},{192,64},{1,129},{65,193},{129,1},{193,65... | collective-permute-start | bytes 712712 | tf_op jit(solution)/shard_map/ppermute | solution.py:185
  57.3 2.5 %collective-permute-start.2 = (bf16[928,128]{1,0:T(8,128)(2,1)S(1)}, bf16[928,128]{1,0:T(8,128)(2,1)S(1)}, u32[]{:S(2)}, u32[]{:S(2)}) collective-permute-start(bf16[928,128]{1,0:T(8,128)(2,1)S(1)} %get-tuple-element.8.refs_0_), channel_id=1, source_target_pairs={{0,64},{64,128},{128,192},{192,0},{1,65},{65,129},{129,193},{193,1... | collective-permute-start | bytes 712712 | tf_op jit(solution)/shard_map/ppermute | solution.py:185
  59.8 4.6 %collective-permute-start.3 = (bf16[928,128]{1,0:T(8,128)(2,1)S(1)}, bf16[928,128]{1,0:T(8,128)(2,1)S(1)}, u32[]{:S(2)}, u32[]{:S(2)}) collective-permute-start(bf16[928,128]{1,0:T(8,128)(2,1)S(1)} %get-tuple-element.8.refs_0_), channel_id=1, source_target_pairs={{0,192},{64,0},{128,64},{192,128},{1,193},{65,1},{129,65},{193,129... | collective-permute-start | bytes 712712 | tf_op jit(solution)/shard_map/ppermute | solution.py:185
  64.4 2.5 %all-gather = bf16[4,928,128]{2,1,0:T(8,128)(2,1)S(1)} all-gather(bf16[2,928,128]{2,1,0:T(8,128)(2,1)S(1)} %get-tuple-element.9), channel_id=2, replica_groups=mesh['enc'=2,'x'=4,'ya'=2,'yb'=2,'core'=2,'za'=4,'zb'=2] {'core'}, dimensions={0}, use_global_device_ids=true | all-gather | bytes 1425408 | tf_op jit(solution)/shard_map/all_gather | solution.py:219
  66.9 2.5 %all-gather.1 = bf16[4,928,128]{2,1,0:T(8,128)(2,1)S(1)} all-gather(bf16[2,928,128]{2,1,0:T(8,128)(2,1)S(1)} %collective-permute-done.1), channel_id=3, replica_groups=mesh['enc'=2,'x'=4,'ya'=2,'yb'=2,'core'=2,'za'=4,'zb'=2] {'core'}, dimensions={0}, use_global_device_ids=true | all-gather | bytes 1425408 | tf_op jit(solution)/shard_map/all_gather | solution.py:219
  69.3 6.1 %flash_third.1 = bf16[144,928]{1,0:T(8,128)(2,1)S(1)} custom-call(s32[3]{0:T(128)S(1)} %pad_add_fusion.place, bf16[928,128]{1,0:T(8,128)(2,1)S(1)} %collective-permute-done.6.refs_0_, bf16[2,2,928,128]{3,2,1,0:T(8,128)(2,1)S(1)} %bitcast.13, bf16[2,2,928,128]{3,2,1,0:T(8,128)(2,1)S(1)} %bitcast.16), custom_call_target="tpu_custom_call" | custom-call | flops 1763704832 | bytes 2405388 | tf_op jit(solution)/shard_map/flash_third/pallas_call | solution.py:32
  75.5 2.1 %collective-permute-start.7 = (bf16[144,928]{1,0:T(8,128)(2,1)S(1)}, bf16[144,928]{1,0:T(8,128)(2,1)S(1)}, u32[]{:S(2)}, u32[]{:S(2)}) collective-permute-start(bf16[144,928]{1,0:T(8,128)(2,1)S(1)} %flash_third.1), channel_id=1, source_target_pairs={{0,128},{64,192},{128,0},{192,64},{1,129},{65,193},{129,1},{193,65... | collective-permute-start | bytes 801800 | tf_op jit(solution)/shard_map/ppermute | solution.py:185
  77.6 0.0 collective-permute-done.3.refs_1_
  77.6 10.7 %flash_two.1 = (bf16[144,928]{1,0:T(8,128)(2,1)S(1)}, bf16[144,928]{1,0:T(8,128)(2,1)S(1)}) custom-call(s32[3]{0:T(128)S(1)} %pad_add_fusion.place, bf16[928,128]{1,0:T(8,128)(2,1)S(1)} %collective-permute-done.2.refs_0_, bf16[928,128]{1,0:T(8,128)(2,1)S(1)} %collective-permute-done.3.refs_1_, bf16[2,2,928,128]{3,2,1,0:T(8,128)(2,1)S(1)} %bitcast.14, ...), custom_call_target="tpu_custom_call" | custom-call | flops 3527409664 | bytes 2910220 | tf_op jit(solution)/shard_map/flash_two/pallas_call | solution.py:32
  88.4 4.0 %collective-permute-start.4 = (bf16[144,928]{1,0:T(8,128)(2,1)S(1)}, bf16[144,928]{1,0:T(8,128)(2,1)S(1)}, u32[]{:S(2)}, u32[]{:S(2)}) collective-permute-start(bf16[144,928]{1,0:T(8,128)(2,1)S(1)} %get-tuple-element.12), channel_id=1, source_target_pairs={{0,192},{64,0},{128,64},{192,128},{1,193},{65,1},{129,65},{193,129... | collective-permute-start | bytes 801800 | tf_op jit(solution)/shard_map/ppermute | solution.py:185
  92.3 2.1 %collective-permute-start.5 = (bf16[144,928]{1,0:T(8,128)(2,1)S(1)}, bf16[144,928]{1,0:T(8,128)(2,1)S(1)}, u32[]{:S(2)}, u32[]{:S(2)}) collective-permute-start(bf16[144,928]{1,0:T(8,128)(2,1)S(1)} %get-tuple-element.13), channel_id=1, source_target_pairs={{0,64},{64,128},{128,192},{192,0},{1,65},{65,129},{129,193},{193,1... | collective-permute-start | bytes 801800 | tf_op jit(solution)/shard_map/ppermute | solution.py:185
  94.5 6.0 %flash_own.1 = (f32[128,928]{1,0:T(8,128)S(1)}, f32[16,928]{1,0:T(8,128)S(1)}) custom-call(s32[3]{0:T(128)S(1)} %pad_add_fusion.place, bf16[928,128]{1,0:T(8,128)(2,1)S(1)} %get-tuple-element.8.refs_0_, bf16[2,2,928,128]{3,2,1,0:T(8,128)(2,1)S(1)} %bitcast.15, bf16[2,2,928,128]{3,2,1,0:T(8,128)(2,1)S(1)} %bitcast.18), custom_call_target="tpu_custom_call" | custom-call | flops 1763704832 | bytes 2672652 | tf_op jit(solution)/shard_map/flash_own/pallas_call | solution.py:32
  100.5 0.0 collective-permute-done.7.got3
  100.5 3.4 %collective-permute-done.5.got2 = bf16[144,928]{1,0:T(8,128)(2,1)S(1)} collective-permute-done((bf16[144,928]{1,0:T(8,128)(2,1)S(1)}, bf16[144,928]{1,0:T(8,128)(2,1)S(1)}, u32[]{:S(2)}, u32[]{:S(2)}) %collective-permute-start.5) | collective-permute-done | bytes 267296 | tf_op jit(solution)/shard_map/ppermute | solution.py:185
  103.9 0.3 merge.1
  104.2 19.0 %all_to_all.11.chunks = bf16[16,64,128]{2,1,0:T(8,128)(2,1)S(1)} all-to-all(bf16[16,64,128]{2,1,0:T(8,128)(2,1)S(1)} %merge.1), channel_id=1, replica_groups=mesh['enc'=2,'x'=4,'ya'=2,'yb'=2,'core'=2,'za'=4,'zb'=2] {'za','ya','yb'}, dimensions={0} | all-to-all | bytes 524288 | tf_op jit(solution)/shard_map/all_to_all | solution.py:242
  123.3 0.7 spread.1
  (12 shorter events, 0.1 us)
Async XLA Ops:
  0.6 0.7 copy-start.5
  0.6 0.7 copy-start.4
  0.7 0.7 copy-start.3
  1.4 10.7 %collective-permute-start = (bf16[3,4,256]{2,1,0:T(4,128)(2,1)S(1)}, bf16[3,4,256]{2,1,0:T(4,128)(2,1)S(1)}, u32[]{:S(2)}, u32[]{:S(2)}) collective-permute-start(bf16[3,4,256]{2,1,0:T(4,128)(2,1)S(1)} %get-tuple-element.15), channel_id=1, source_target_pairs={{0,256},{256,0},{1,257},{257,1},{2,258},{258,2},{3,259},{259,3},{4... | collective-permute-start | bytes 18440 | tf_op jit(solution)/shard_map/ppermute | solution.py:185
  9.1 0.9 copy-start
  10.1 0.9 copy-start.1
  11.0 0.9 copy-start.2
  48.8 18.0 %collective-permute-start.1 = (bf16[2,928,128]{2,1,0:T(8,128)(2,1)S(1)}, bf16[2,928,128]{2,1,0:T(8,128)(2,1)S(1)}, u32[]{:S(2)}, u32[]{:S(2)}) collective-permute-start(bf16[2,928,128]{2,1,0:T(8,128)(2,1)S(1)} %get-tuple-element.9), channel_id=1, source_target_pairs={{0,1},{1,0},{2,3},{3,2},{4,5},{5,4},{6,7},{7,6},{8,9},{9,8},{10,11... | collective-permute-start | bytes 1425416 | tf_op jit(solution)/shard_map/ppermute | solution.py:185
  52.4 17.0 %collective-permute-start.6 = (bf16[928,128]{1,0:T(8,128)(2,1)S(1)}, bf16[928,128]{1,0:T(8,128)(2,1)S(1)}, u32[]{:S(2)}, u32[]{:S(2)}) collective-permute-start(bf16[928,128]{1,0:T(8,128)(2,1)S(1)} %get-tuple-element.8.refs_0_), channel_id=1, source_target_pairs={{0,128},{64,192},{128,0},{192,64},{1,129},{65,193},{129,1},{193,65... | collective-permute-start | bytes 712712 | tf_op jit(solution)/shard_map/ppermute | solution.py:185
  57.3 20.3 %collective-permute-start.2 = (bf16[928,128]{1,0:T(8,128)(2,1)S(1)}, bf16[928,128]{1,0:T(8,128)(2,1)S(1)}, u32[]{:S(2)}, u32[]{:S(2)}) collective-permute-start(bf16[928,128]{1,0:T(8,128)(2,1)S(1)} %get-tuple-element.8.refs_0_), channel_id=1, source_target_pairs={{0,64},{64,128},{128,192},{192,0},{1,65},{65,129},{129,193},{193,1... | collective-permute-start | bytes 712712 | tf_op jit(solution)/shard_map/ppermute | solution.py:185
  59.8 17.8 %collective-permute-start.3 = (bf16[928,128]{1,0:T(8,128)(2,1)S(1)}, bf16[928,128]{1,0:T(8,128)(2,1)S(1)}, u32[]{:S(2)}, u32[]{:S(2)}) collective-permute-start(bf16[928,128]{1,0:T(8,128)(2,1)S(1)} %get-tuple-element.8.refs_0_), channel_id=1, source_target_pairs={{0,192},{64,0},{128,64},{192,128},{1,193},{65,1},{129,65},{193,129... | collective-permute-start | bytes 712712 | tf_op jit(solution)/shard_map/ppermute | solution.py:185
  75.5 25.0 %collective-permute-start.7 = (bf16[144,928]{1,0:T(8,128)(2,1)S(1)}, bf16[144,928]{1,0:T(8,128)(2,1)S(1)}, u32[]{:S(2)}, u32[]{:S(2)}) collective-permute-start(bf16[144,928]{1,0:T(8,128)(2,1)S(1)} %flash_third.1), channel_id=1, source_target_pairs={{0,128},{64,192},{128,0},{192,64},{1,129},{65,193},{129,1},{193,65... | collective-permute-start | bytes 801800 | tf_op jit(solution)/shard_map/ppermute | solution.py:185
  88.4 12.2 %collective-permute-start.4 = (bf16[144,928]{1,0:T(8,128)(2,1)S(1)}, bf16[144,928]{1,0:T(8,128)(2,1)S(1)}, u32[]{:S(2)}, u32[]{:S(2)}) collective-permute-start(bf16[144,928]{1,0:T(8,128)(2,1)S(1)} %get-tuple-element.12), channel_id=1, source_target_pairs={{0,192},{64,0},{128,64},{192,128},{1,193},{65,1},{129,65},{193,129... | collective-permute-start | bytes 801800 | tf_op jit(solution)/shard_map/ppermute | solution.py:185
  92.3 11.6 %collective-permute-start.5 = (bf16[144,928]{1,0:T(8,128)(2,1)S(1)}, bf16[144,928]{1,0:T(8,128)(2,1)S(1)}, u32[]{:S(2)}, u32[]{:S(2)}) collective-permute-start(bf16[144,928]{1,0:T(8,128)(2,1)S(1)} %get-tuple-element.13), channel_id=1, source_target_pairs={{0,64},{64,128},{128,192},{192,0},{1,65},{65,129},{129,193},{193,1... | collective-permute-start | bytes 801800 | tf_op jit(solution)/shard_map/ppermute | solution.py:185
